TPU v7x, 128 devices: a whole 4x4x4 slice. The times are simulated.
128 devices in a mesh: row: 8 (over y_lo, z), col: 16 (over x, y_hi, core).
Axes of the slice: x: 4, y: 4 (y_hi: 2, y_lo: 2; y = y_hi * 2 + y_lo), z: 4, core: 2. Of those that a mesh axis runs over, the one named last changes fastest.
Arguments:
- pair: float32 [512, 512, 128], P('row', 'col'), may hold values from -6 to 6
- norm_gain: float32 [2, 2, 128], replicated, may hold values from 0.1 to 1.9
- proj_weight: bfloat16 [2, 128, 640], replicated, may hold values from -0.5 to 0.5
- out_weight: bfloat16 [2, 128, 128], replicated, may hold values from -0.5 to 0.5
Outputs:
- updated_pair: float32 [512, 512, 128], P('row', 'col')
All inputs are finite; a program needn't handle non-finite values.
Results may differ from a plain program's by a relative error of at most 0.0055.
Values may be sent and summed in bfloat16 or wider, within the bound.
A program may use at most 128 MiB of HBM per device.

v0:
```python
import jax
import jax.numpy as jnp
from jax import lax
from jax.sharding import PartitionSpec as P


def layer_norm(values, scale_gain):
    center = jnp.mean(values, axis=-1, keepdims=True)
    shifted = values - center
    spread = jnp.mean(shifted * shifted, axis=-1, keepdims=True)
    return shifted * lax.rsqrt(spread + 1e-05) * scale_gain


def project_pair(pair_state, scale_gain, proj_matrix):
    rows, cols, chan = pair_state.shape
    hidden = proj_matrix.shape[1] // 5
    normed = layer_norm(pair_state, scale_gain).astype(jnp.bfloat16).reshape(rows * cols, chan)
    proj = jnp.dot(normed, proj_matrix, preferred_element_type=jnp.float32).reshape(
        rows, cols, 5 * hidden
    )
    left_edge = (jax.nn.sigmoid(proj[..., 0:hidden]) * proj[..., hidden : 2 * hidden]).astype(
        jnp.bfloat16
    )
    right_edge = (
        jax.nn.sigmoid(proj[..., 2 * hidden : 3 * hidden]) * proj[..., 3 * hidden : 4 * hidden]
    ).astype(jnp.bfloat16)
    out_gate = jax.nn.sigmoid(proj[..., 4 * hidden : 5 * hidden])
    return (left_edge, right_edge, out_gate)


def finish_update(pair_state, product, scale_gain, out_matrix, out_gate):
    rows, cols, hidden = product.shape
    outnorm = layer_norm(product, scale_gain).astype(jnp.bfloat16).reshape(rows * cols, hidden)
    mapped = jnp.dot(outnorm, out_matrix, preferred_element_type=jnp.float32).reshape(
        rows, cols, -1
    )
    return pair_state + out_gate * mapped


def shards(pair, norm_gain, proj_weight, out_weight):
    state = pair
    left_edge, right_edge, out_gate = project_pair(state, norm_gain[0, 0], proj_weight[0])
    right_rows = lax.all_gather(right_edge, "row", axis=0, tiled=True)
    right_mine = lax.all_to_all(right_rows, "col", split_axis=0, concat_axis=1, tiled=True)
    matching = right_mine
    product = jnp.einsum(
        "ikc,jkc->ijc",
        lax.all_gather(left_edge, "col", axis=1, tiled=True),
        matching,
        preferred_element_type=jnp.float32,
    )
    state = finish_update(state, product, norm_gain[0, 1], out_weight[0], out_gate)
    left_edge, right_edge, out_gate = project_pair(state, norm_gain[1, 0], proj_weight[1])
    left_cols = lax.all_gather(left_edge, "col", axis=1, tiled=True)
    left_mine = lax.all_to_all(left_cols, "row", split_axis=1, concat_axis=0, tiled=True)
    matching = left_mine
    product = jnp.einsum(
        "kic,kjc->ijc",
        matching,
        lax.all_gather(right_edge, "row", axis=0, tiled=True),
        preferred_element_type=jnp.float32,
    )
    state = finish_update(state, product, norm_gain[1, 1], out_weight[1], out_gate)
    return state


def solution(mesh):
    placed = (P("row", "col", None), P(), P(), P())
    return jax.shard_map(
        shards, mesh=mesh, in_specs=placed, out_specs=P("row", "col", None), check_vma=False
    )
```

profile of v0, /device:TPU:1, one launch (start us, length us, event | category | flops | bytes accessed | tf_op | source)
XLA Modules:
  0.0 501.3 jit_solution(5478082099454927378)
XLA Ops:
  6.5 0.8 slice_bitcast_fusion
  7.3 1.6 reduce_sum.72
  8.9 0.1 copy.70
  8.9 0.1 copy.71
  9.0 1.9 multiply_reduce_fusion.3
  10.9 0.1 copy.72
  11.0 0.1 copy.73
  11.1 2.4 fusion.24
  13.4 2.4 copy-done.1
  15.8 1.5 fusion.13
  17.3 0.0 all-gather.5.cloned.1.call-update
  17.3 0.0 all-gather.7.cloned.1.call-start
  17.4 0.7 all-gather.7.cloned.1.call-update
  18.1 0.0 all-gather.11.cloned.1.call-start
  18.1 55.4 %all-gather.5.cloned.1.call-done = bf16[512,32,128]{2,1,0:T(8,128)(2,1)} async-done(((bf16[64,32,128]{2,1,0:T(8,128)(2,1)}), bf16[512,32,128]{2,1,0:T(8,128)(2,1)}) %all-gather.5.cloned.1.call-update) | async-done | bytes 4194320 | tf_op jit(solution)/shard_map/all_gather | solution.py:43
  73.5 66.0 %all_to_all.36 = bf16[512,32,128]{2,1,0:T(8,128)(2,1)S(1)} all-to-all(bf16[512,32,128]{2,1,0:T(8,128)(2,1)} %all-gather.5.cloned.1.call-done), channel_id=1, replica_groups=mesh['row'=8,'col'=16] {'col'}, dimensions={0} | all-to-all | bytes 8388608 | tf_op jit(solution)/shard_map/all_to_all | solution.py:44
  139.5 3.2 copy.74
  142.7 8.0 %copy.75 = bf16[32,512,128]{1,0,2:T(8,128)(2,1)} copy(bf16[32,512,128]{2,1,0:T(8,128)(2,1)} %bitcast.56) | data formatting | bytes 8388608 | tf_op jit(solution)/shard_map/all_to_all | solution.py:44
  150.7 31.3 %all-gather.7.cloned.1.call-done = bf16[64,512,128]{2,1,0:T(8,128)(2,1)} async-done(((bf16[64,32,128]{2,1,0:T(8,128)(2,1)}), bf16[64,512,128]{2,1,0:T(8,128)(2,1)}) %all-gather.7.cloned.1.call-update) | async-done | bytes 8388624 | tf_op jit(solution)/shard_map/all_gather | solution.py:48
  182.0 29.2 %copy.76 = bf16[64,512,128]{0,1,2:T(8,128)(2,1)} copy(bf16[64,512,128]{2,1,0:T(8,128)(2,1)} %all-gather.7.cloned.1.call-done) | data formatting | bytes 16777216 | tf_op jit(solution)/shard_map/all_gather | solution.py:48
  211.1 9.7 %bitcast_reduce_fusion.1 = (f32[64,32]{0,1:T(8,128)S(1)}, f32[128,32,64]{2,1,0:T(8,128)S(1)}) fusion(bf16[32,512,128]{1,0,2:T(8,128)(2,1)} %copy.75, bf16[64,512,128]{0,1,2:T(8,128)(2,1)} %copy.76), kind=kOutput, calls=%fused_computation.3 | convolution fusion | flops 268695552 | bytes 13639680 | tf_op jit(solution)/shard_map/ikc,jkc->ijc/dot_general | solution.py:46
  220.9 0.3 multiply_reduce_fusion.1
  221.2 0.3 multiply_convert_fusion.1
  221.5 1.5 copy.77
  223.1 1.7 fusion.40
  224.9 0.1 copy.78
  224.9 0.1 copy.79
  225.0 0.6 multiply_reduce_fusion.2
  225.7 0.1 copy.80
  225.8 0.1 copy.81
  225.9 1.0 fusion.25
  226.9 2.3 copy-done
  229.2 1.5 fusion.2
  230.7 0.0 all-gather.11.cloned.1.call-update
  230.7 0.3 all-gather.9.cloned.1.call-start
  231.0 0.3 all-gather.9.cloned.1.call-update
  231.3 78.1 %all-gather.11.cloned.1.call-done = bf16[64,512,128]{2,1,0:T(8,128)(2,1)} async-done(((bf16[64,32,128]{2,1,0:T(8,128)(2,1)}), bf16[64,512,128]{2,1,0:T(8,128)(2,1)}) %all-gather.11.cloned.1.call-update) | async-done | bytes 8388624 | tf_op jit(solution)/shard_map/all_gather | solution.py:54
  309.5 12.0 %copy.82 = bf16[64,512,128]{2,0,1:T(8,128)(2,1)} copy(bf16[64,512,128]{2,1,0:T(8,128)(2,1)} %all-gather.11.cloned.1.call-done) | data formatting | bytes 16777216 | tf_op jit(solution)/shard_map/all_gather | solution.py:54
  321.4 5.2 %all-to-all-start.1 = ((bf16[64,512,128]{2,0,1:T(8,128)(2,1)}), bf16[64,512,128]{2,0,1:T(8,128)(2,1)}, u32[]{:S(2)}, u32[]{:S(2)}) async-start(bf16[64,512,128]{2,0,1:T(8,128)(2,1)} %copy.82), calls=%async_computation.1 | async-start | bytes 16777216 | tf_op jit(solution)/shard_map/all_to_all | solution.py:55
  326.7 122.2 %all-gather.9.cloned.1.call-done = bf16[512,32,128]{2,1,0:T(8,128)(2,1)} async-done(((bf16[64,32,128]{2,1,0:T(8,128)(2,1)}), bf16[512,32,128]{2,1,0:T(8,128)(2,1)}) %all-gather.9.cloned.1.call-update) | async-done | bytes 4194320 | tf_op jit(solution)/shard_map/all_gather | solution.py:60
  448.9 8.6 %copy.85 = bf16[512,32,128]{0,1,2:T(8,128)(2,1)} copy(bf16[512,32,128]{2,1,0:T(8,128)(2,1)} %all-gather.9.cloned.1.call-done) | data formatting | bytes 8388608 | tf_op jit(solution)/shard_map/all_gather | solution.py:60
  457.5 12.0 %copy.84 = bf16[8,64,64,128]{3,2,1,0:T(8,128)(2,1)} copy(bf16[8,64,64,128]{3,1,2,0:T(8,128)(2,1)} %bitcast.15) | data formatting | bytes 16777216 | tf_op jit(solution)/shard_map/all_to_all | solution.py:55
  469.5 13.5 %copy.86 = bf16[512,64,128]{0,1,2:T(8,128)(2,1)} copy(bf16[512,64,128]{2,1,0:T(8,128)(2,1)} %bitcast.54) | data formatting | bytes 16777216 | tf_op jit(solution)/shard_map/all_to_all | solution.py:55
  483.0 7.0 %bitcast_reduce_fusion = (f32[64,32]{0,1:T(8,128)S(1)}, f32[128,32,64]{2,1,0:T(8,128)S(1)}) fusion(bf16[512,32,128]{0,1,2:T(8,128)(2,1)} %copy.85, bf16[512,64,128]{0,1,2:T(8,128)(2,1)} %copy.86), kind=kOutput, calls=%fused_computation.1 | convolution fusion | flops 268695552 | bytes 13639680 | tf_op jit(solution)/shard_map/kic,kjc->ijc/dot_general | solution.py:57
  490.0 0.3 multiply_reduce_fusion
  490.3 0.3 multiply_convert_fusion
  490.7 1.5 copy.87
  492.2 2.6 fusion
  (18 shorter events, 0.1 us)
Async XLA Ops:
  6.5 67.0 %all-gather.5.cloned.1.call-start = ((), (), s32[]{:S(2)}) async-start(), calls=%async_computation.2 | async-start | bytes 4718592 | tf_op jit(solution)/shard_map/all_gather | solution.py:43
  13.4 2.4 copy-start.1
  17.3 164.6 %all-gather.7.cloned.1.call-start = ((), (), s32[]{:S(2)}) async-start(), calls=%async_computation.3 | async-start | bytes 8912896 | tf_op jit(solution)/shard_map/all_gather | solution.py:48
  18.1 291.4 %all-gather.11.cloned.1.call-start = ((), (), s32[]{:S(2)}) async-start(), calls=%async_computation.5 | async-start | bytes 8912896 | tf_op jit(solution)/shard_map/all_gather | solution.py:54
  220.8 2.3 copy-start.2
  220.8 2.3 copy-start.4
  221.5 4.3 copy-start.3
  226.9 2.3 copy-start
  230.7 218.1 %all-gather.9.cloned.1.call-start = ((), (), s32[]{:S(2)}) async-start(), calls=%async_computation.4 | async-start | bytes 4718592 | tf_op jit(solution)/shard_map/all_gather | solution.py:60
  321.4 136.0 %all-to-all-start.1 = ((bf16[64,512,128]{2,0,1:T(8,128)(2,1)}), bf16[64,512,128]{2,0,1:T(8,128)(2,1)}, u32[]{:S(2)}, u32[]{:S(2)}) async-start(bf16[64,512,128]{2,0,1:T(8,128)(2,1)} %copy.82), calls=%async_computation.1 | async-start | bytes 16777216 | tf_op jit(solution)/shard_map/all_to_all | solution.py:55
Sparse Core Ops, SparseCore 0:
  17.5 56.0 all-gather.4
  75.8 106.1 all-gather.6
  230.9 78.5 all-gather.10
  311.0 137.8 all-gather.8
where the time goes:
time: 508 us; the launch traced here: 501 us
  waiting for transfers between devices  288 us (57%)
  local copies, waits for them, and re-layouts  95.6 us (19%)
  blocking collectives  66 us (13%)
  matrix products  24.3 us (5%)
  between operations  13.3 us (3%)
  other arithmetic  8.52 us (2%)
  starting transfers between devices  5.55 us (1%)
    all_gather x1, waiting for transfers between devices, shards(): lax.all_gather(right_edge, 'row', axis=0, tiled=True)  122 us
    all_gather x1, waiting for transfers between devices, shards(): left_cols = lax.all_gather(left_edge, 'col', axis=1, tiled=True)  78.1 us
    all_to_all x1, blocking collectives, shards(): lax.all_to_all(right_rows, 'col', split_axis=0, concat_axis=1, tiled=True)  66 us
    all_gather x1, waiting for transfers between devices, shards(): right_rows = lax.all_gather(right_edge, 'row', axis=0, tiled=True)  55.4 us
    all_gather x1, waiting for transfers between devices, shards(): lax.all_gather(left_edge, 'col', axis=1, tiled=True)  31.3 us
    all_gather x1, local copies, waits for them, and re-layouts, shards(): lax.all_gather(left_edge, 'col', axis=1, tiled=True)  29.2 us
    all_to_all x2, local copies, waits for them, and re-layouts, shards(): lax.all_to_all(left_cols, 'row', split_axis=1, concat_axis=0, tiled=True)  25.5 us
    all_gather x1, local copies, waits for them, and re-layouts, shards(): left_cols = lax.all_gather(left_edge, 'col', axis=1, tiled=True)  12 us
  transfers between devices with their start and end apart: 5, of which 4 were waited for; matrix products, arithmetic and copies ran while one was open for 6% of the time, Pallas kernels for 0%

commit v1 on v0

v1 whole, which is shorter than its diff:
```python
import functools

import jax
import jax.numpy as jnp
from jax import lax
from jax.experimental import pallas as pl
from jax.experimental.pallas import tpu as pltpu
from jax.sharding import PartitionSpec as P

MESH = pl.DeviceIdType.MESH
ROWS, COLS = 8, 16
DEV = ROWS * COLS
A, B = 64, 32
CH = 128
POS = A * B
TILES = 16
N = 512


def sigmoid(x):
    return 0.5 * jnp.tanh(0.5 * x) + 0.5


def layer_norm(x):
    center = jnp.mean(x, axis=-1, keepdims=True)
    shifted = x - center
    spread = jnp.mean(shifted * shifted, axis=-1, keepdims=True)
    return shifted * lax.rsqrt(spread + 1e-05)


def swap_halves(v0, v1):
    h = CH // 2
    return (
        jnp.concatenate([v0[:, :h], v1[:, :h]], axis=1),
        jnp.concatenate([v0[:, h:], v1[:, h:]], axis=1),
    )


def kernel(pair, gain, weight, weight_out, out, state, normed, gate, wt, wide, send, recv, xl, xr,
           tri_send, tri_recv, stats, send_sem, recv_sem):
    r, c = lax.axis_index("row"), lax.axis_index("col")
    me = r * COLS + c

    def partner(t):
        d = lax.rem(me + t, DEV)
        return d, (lax.div(d, COLS), lax.rem(d, COLS))

    barrier = pltpu.get_barrier_semaphore()

    def greet(t, _):
        pl.semaphore_signal(barrier, inc=1, device_id=partner(t)[1], device_id_type=MESH)
        return 0

    lax.fori_loop(1, DEV, greet, 0)

    def exchange(src, dst, step):
        def send_one(t, _):
            d, dev = partner(t)
            pltpu.make_async_remote_copy(
                src_ref=src.at[d], dst_ref=dst.at[me], send_sem=send_sem.at[step],
                recv_sem=recv_sem.at[step], device_id=dev, device_id_type=MESH,
            ).start()
            return 0

        lax.fori_loop(1, DEV, send_one, 0)
        pltpu.make_async_copy(src.at[me], dst.at[me], recv_sem.at[step]).start()

    def arrived(dst, step):
        pltpu.make_async_copy(dst, dst, recv_sem.at[step]).wait()

    def left(src, step):
        rest = src.at[pl.ds(0, DEV - 1)]
        pltpu.make_async_copy(rest, rest, send_sem.at[step]).wait()

    for s in range(TILES):
        for p in range(2):
            state[pl.ds(s * CH + p * A, A), :] = pair[pl.ds(p * TILES + s, A, stride=B), :]

    for u in range(2):
        wt[...] = jnp.transpose(weight[u, :, 0 : 4 * CH])

        def project(n, _):
            at = pl.ds(pl.multiple_of(n * 256, 256), 256)
            rows = (layer_norm(state[at, :]) * gain[2 * u : 2 * u + 1, :]).astype(jnp.bfloat16)
            normed[at, :] = rows
            proj = lax.dot_general(
                wt[...], rows, (((1,), (1,)), ((), ())), preferred_element_type=jnp.float32
            )
            le = sigmoid(proj[0:CH]) * proj[CH : 2 * CH]
            ri = sigmoid(proj[2 * CH : 3 * CH]) * proj[3 * CH : 4 * CH]
            for h in range(2):
                s = n * 2 + h
                wide[pl.ds(s, CH, stride=32), :] = le[:, h * CH : (h + 1) * CH]
                wide[pl.ds(TILES + s, CH, stride=32), :] = ri[:, h * CH : (h + 1) * CH]
            return 0

        lax.fori_loop(0, 8, project, 0)
        if u == 0:
            pl.semaphore_wait(barrier, DEV - 1)
        else:
            left(send, 0)

        def pack(n, _):
            send[pl.ds(n * 16, 16)] = (
                wide[pl.ds(pl.multiple_of(n * 512, 512), 512), :].astype(jnp.bfloat16).reshape(16, 32, CH)
            )
            return 0

        lax.fori_loop(0, 8, pack, 0)
        exchange(send, recv.at[u], 2 * u)

        def open_gate(n, _):
            at = pl.ds(pl.multiple_of(n * 256, 256), 256)
            gate[at, :] = sigmoid(
                jnp.dot(normed[at, :], weight[u, :, 4 * CH : 5 * CH], preferred_element_type=jnp.float32)
            )
            return 0

        lax.fori_loop(0, 8, open_gate, 0)
        gain_out = jnp.transpose(jnp.broadcast_to(gain[2 * u + 1 : 2 * u + 2, :], (CH, CH)))
        arrived(recv.at[u], 2 * u)

        def join(cc, _):
            for rp in range(4):
                t0 = recv[u, 2 * rp * COLS + cc]
                t1 = recv[u, (2 * rp + 1) * COLS + cc]
                for x, lo in ((xl, 0), (xr, TILES)):
                    p0, p1 = swap_halves(t0[lo : lo + TILES], t1[lo : lo + TILES])
                    x[pl.ds(pl.multiple_of(cc * B, B), TILES), rp * CH : (rp + 1) * CH] = p0
                    x[pl.ds(pl.multiple_of(cc * B + TILES, TILES), TILES), rp * CH : (rp + 1) * CH] = p1
            return 0

        lax.fori_loop(0, COLS, join, 0)

        over = 0 if u == 0 else 1
        if u == 1:
            left(tri_send, 1)
        for h in range(4):
            if u == 0:
                lhs = xr[:, h * CH : (h + 1) * CH]
            else:
                lhs = xr[h * CH : (h + 1) * CH, :]
            tri = lax.dot_general(
                lhs, xl[...], (((over,), (over,)), ((), ())), preferred_element_type=jnp.float32
            ).astype(jnp.bfloat16)
            for i in range(4):
                cc = h * 4 + i
                for rp in range(4):
                    q0 = tri[i * B : i * B + TILES, rp * CH : (rp + 1) * CH]
                    q1 = tri[i * B + TILES : (i + 1) * B, rp * CH : (rp + 1) * CH]
                    p0, p1 = swap_halves(q0, q1)
                    tri_send[2 * rp * COLS + cc] = p0
                    tri_send[(2 * rp + 1) * COLS + cc] = p1
        exchange(tri_send, tri_recv.at[u], 2 * u + 1)
        arrived(tri_recv.at[u], 2 * u + 1)

        def add(n, acc):
            return acc + tri_recv[u, pl.ds(n * 8, 8)].astype(jnp.float32).sum(axis=0)

        center = lax.fori_loop(0, 16, add, jnp.zeros((TILES, CH), jnp.float32)) * (1.0 / CH)

        def add_square(n, acc):
            x = tri_recv[u, pl.ds(n * 8, 8)].astype(jnp.float32) - center
            return acc + (x * x).sum(axis=0)

        spread = lax.fori_loop(0, 16, add_square, jnp.zeros((TILES, CH), jnp.float32)) * (1.0 / CH)
        inv = lax.rsqrt(spread + 1e-05)

        def scale(n, _):
            x = (tri_recv[u, pl.ds(n * 8, 8)].astype(jnp.float32) - center) * inv
            wide[pl.ds(pl.multiple_of(n * 128, 128), 128), :] = x.reshape(8 * TILES, CH)
            return 0

        lax.fori_loop(0, 16, scale, 0)
        stats[...] = gain_out
        for s in range(TILES):
            outnorm = (wide[pl.ds(s, CH, stride=TILES), :] * stats[...]).astype(jnp.bfloat16)
            mapped = lax.dot_general(
                outnorm, weight_out[u], (((0,), (0,)), ((), ())), preferred_element_type=jnp.float32
            )
            at = pl.ds(s * CH, CH)
            new = state[at, :] + gate[at, :] * mapped
            if u == 0:
                state[at, :] = new
            else:
                for p in range(2):
                    out[pl.ds(p * TILES + s, A, stride=B), :] = new[p * A : (p + 1) * A]
    left(send, 2)
    left(tri_send, 3)


def shards(pair, gain, weight, weight_out):
    vmem = pl.BlockSpec(memory_space=pltpu.VMEM)
    f32, bf16 = jnp.float32, jnp.bfloat16
    result = pl.pallas_call(
        kernel,
        out_shape=jax.ShapeDtypeStruct((POS, CH), f32),
        in_specs=[vmem] * 4,
        out_specs=vmem,
        scratch_shapes=[
            pltpu.VMEM((POS, CH), f32),
            pltpu.VMEM((POS, CH), bf16),
            pltpu.VMEM((POS, CH), f32),
            pltpu.VMEM((4 * CH, CH), bf16),
            pltpu.VMEM((2 * POS, CH), f32),
            pltpu.VMEM((DEV, 2 * TILES, CH), bf16),
            pltpu.VMEM((2, DEV, 2 * TILES, CH), bf16),
            pltpu.VMEM((N, N), bf16),
            pltpu.VMEM((N, N), bf16),
            pltpu.VMEM((DEV, TILES, CH), bf16),
            pltpu.VMEM((2, DEV, TILES, CH), bf16),
            pltpu.VMEM((CH, CH), f32),
            pltpu.SemaphoreType.DMA((4,)),
            pltpu.SemaphoreType.DMA((4,)),
        ],
        compiler_params=pltpu.CompilerParams(
            collective_id=0, has_side_effects=True, vmem_limit_bytes=40 << 20
        ),
    )(pair.reshape(POS, CH), gain.reshape(4, CH), weight, weight_out)
    return result.reshape(A, B, CH)


def solution(mesh):
    placed = (P("row", "col", None), P(), P(), P())
    return jax.shard_map(
        shards, mesh=mesh, in_specs=placed, out_specs=P("row", "col", None), check_vma=False
    )
```

time: 508 us -> 79 us (0.16); the launches traced: 501 us -> 78.7 us
  waiting for transfers between devices: 288 us -> 0 us
  local copies, waits for them, and re-layouts: 95.6 us -> 4.69 us
  Pallas kernels: 0 us -> 74 us
  blocking collectives: 66 us -> 0 us
  matrix products: 24.3 us -> 0 us
  between operations: 13.3 us -> 0.01 us
  other arithmetic: 8.52 us -> 0 us
  starting transfers between devices: 5.55 us -> 0 us
    all_gather x4 -> x0, waiting for transfers between devices: 287 us -> none  [the longest x1 122 us: shards(): lax.all_gather(right_edge, 'row', axis=0, tiled=True)]
    pallas_call x0 -> x1, Pallas kernels: none -> 74 us  [shards(): pl.pallas_call(kernel, out_shape=jax.ShapeDtypeStruct((POS, CH), f32), in...]
    all_to_all x1 -> x0, blocking collectives: 66 us -> none  [shards(): lax.all_to_all(right_rows, 'col', split_axis=0, concat_axis=1, tiled=True)]
    all_gather x3 -> x0, local copies, waits for them, and re-layouts: 49.8 us -> none  [the longest x1 29.2 us: shards(): lax.all_gather(left_edge, 'col', axis=1, tiled=True)]
    all_to_all x4 -> x0, local copies, waits for them, and re-layouts: 36.7 us -> none  [the longest x2 25.5 us: shards(): lax.all_to_all(left_cols, 'row', split_axis=1, concat_axis=0, tiled=True)]
    dot_general x6 -> x0, matrix products: 24.3 us -> none  [the longest x1 9.67 us: shards(): jnp.einsum('ikc,jkc->ijc', lax.all_gather(left_edge, 'col', axis=1, tiled...]
    all_to_all x1 -> x0, starting transfers between devices: 5.21 us -> none  [shards(): lax.all_to_all(left_cols, 'row', split_axis=1, concat_axis=0, tiled=True)]
  transfers between devices with their start and end apart: 5 -> 0, of which waited for: 4 -> 0; matrix products, arithmetic and copies ran while one was open for 6% -> 0% of each run, Pallas kernels for 0% -> 0%
where the time goes in v1:
time: 79 us; the launch traced here: 78.7 us
  Pallas kernels  74 us (94%)
  local copies, waits for them, and re-layouts  4.69 us (6%)
    pallas_call x1, Pallas kernels, shards(): pl.pallas_call(kernel, out_shape=jax.ShapeDtypeStruct((POS, CH), f32), in...  74 us
    unnamed x9, local copies, waits for them, and re-layouts  4.69 us

profile of v1, /device:TPU:1, one launch (start us, length us, event | category | flops | bytes accessed | tf_op | source)
XLA Modules:
  0.0 78.7 jit_solution(2049804440070060090)
XLA Ops:
  0.0 0.0 copy-start.3
  0.0 0.7 copy-done.3
  0.7 0.0 copy-start
  0.7 1.2 %copy-done = f32[64,32,128]{2,1,0:T(8,128)S(1)} copy-done((f32[64,32,128]{2,1,0:T(8,128)S(1)}, f32[64,32,128]{2,1,0:T(8,128)}, u32[]{:S(2)}) %copy-start) | copy-done | bytes 1048600
  1.9 0.0 copy-start.1
  1.9 1.0 %copy-done.1 = bf16[2,128,640]{2,1,0:T(8,128)(2,1)S(1)} copy-done((bf16[2,128,640]{2,1,0:T(8,128)(2,1)S(1)}, bf16[2,128,640]{2,1,0:T(8,128)(2,1)}, u32[]{:S(2)}) %copy-start.1) | copy-done | bytes 327704
  2.9 0.0 copy-start.2
  2.9 0.8 %copy-done.2 = bf16[2,128,128]{2,1,0:T(8,128)(2,1)S(1)} copy-done((bf16[2,128,128]{2,1,0:T(8,128)(2,1)S(1)}, bf16[2,128,128]{2,1,0:T(8,128)(2,1)}, u32[]{:S(2)}) %copy-start.2) | copy-done | bytes 65560
  3.7 74.0 %shard_map.46 = f32[2048,128]{1,0:T(8,128)S(1)} custom-call(f32[2048,128]{1,0:T(8,128)S(1)} %bitcast.4, f32[4,128]{1,0:T(4,128)S(1)} %bitcast.5, bf16[2,128,640]{2,1,0:T(8,128)(2,1)S(1)} %copy-done.1, bf16[2,128,128]{2,1,0:T(8,128)(2,1)S(1)} %copy-done.2), custom_call_target="tpu_custom_call" | custom-call | tf_op jit(solution)/shard_map/pallas_call | solution.py:195
  77.8 1.0 %copy.6 = f32[64,32,128]{2,1,0:T(8,128)} copy(f32[64,32,128]{2,1,0:T(8,128)S(1)} %bitcast.3) | data formatting | bytes 2097152
Async XLA Ops:
  0.0 0.7 copy-start.3
  0.7 1.2 %copy-start = (f32[64,32,128]{2,1,0:T(8,128)S(1)}, f32[64,32,128]{2,1,0:T(8,128)}, u32[]{:S(2)}) copy-start(f32[64,32,128]{2,1,0:T(8,128)} %param.4) | copy-start | bytes 3145732
  1.9 1.0 %copy-start.1 = (bf16[2,128,640]{2,1,0:T(8,128)(2,1)S(1)}, bf16[2,128,640]{2,1,0:T(8,128)(2,1)}, u32[]{:S(2)}) copy-start(bf16[2,128,640]{2,1,0:T(8,128)(2,1)} %weight.1) | copy-start | bytes 983044
  2.9 0.8 %copy-start.2 = (bf16[2,128,128]{2,1,0:T(8,128)(2,1)S(1)}, bf16[2,128,128]{2,1,0:T(8,128)(2,1)}, u32[]{:S(2)}) copy-start(bf16[2,128,128]{2,1,0:T(8,128)(2,1)} %weight_out.1) | copy-start | bytes 196612

commit v2 on v1

v2 whole, which is shorter than its diff:
```python
import jax
import jax.numpy as jnp
from jax import lax
from jax.experimental import pallas as pl
from jax.experimental.pallas import tpu as pltpu
from jax.sharding import PartitionSpec as P

MESH = pl.DeviceIdType.MESH
ROWS, COLS = 8, 16
DEV = ROWS * COLS
CHIPS = DEV // 2
A, B = 64, 32
CH = 128
POS = A * B
TILES = 16
N = 512
GROUPS = 2
PER = CH // GROUPS
WIDE = 512
STEPS = POS // WIDE
SUB = WIDE // CH


def sigmoid(x):
    return 0.5 * jnp.tanh(0.5 * x) + 0.5


def layer_norm(x, gain):
    center = jnp.mean(x, axis=0, keepdims=True)
    shifted = x - center
    spread = jnp.mean(shifted * shifted, axis=0, keepdims=True)
    return shifted * lax.rsqrt(spread + 1e-05) * gain


def swap_halves(v0, v1):
    h = CH // 2
    return (
        jnp.concatenate([v0[:, :h], v1[:, :h]], axis=1),
        jnp.concatenate([v0[:, h:], v1[:, h:]], axis=1),
    )


def dot(a, b):
    return jnp.dot(a, b, preferred_element_type=jnp.float32)


def kernel(pair_in, gain_in, weight_in, weight_out_in, out, pair, gain, weight, weight_out, state,
           normed, gate, wt, wot, gcol, wide, send, recv, xl, xr, tri_send, tri_recv, in_sem,
           send_sem, recv_sem, met_sem):
    r, c = lax.axis_index("row"), lax.axis_index("col")
    me = r * COLS + c
    chip, core = lax.div(me, 2), lax.rem(me, 2)
    mine = core * PER + chip

    loads = [
        pltpu.make_async_copy(x, y, in_sem.at[i])
        for i, (x, y) in enumerate(
            ((weight_in, weight), (gain_in, gain), (pair_in, pair), (weight_out_in, weight_out))
        )
    ]
    for load in loads:
        load.start()

    barrier = pltpu.get_barrier_semaphore()
    for t in range(1, ROWS):
        pl.semaphore_signal(barrier, inc=1, device_id=(lax.rem(r + t, ROWS), c), device_id_type=MESH)
    for t in range(1, COLS):
        pl.semaphore_signal(barrier, inc=1, device_id=(r, lax.rem(c + t, COLS)), device_id_type=MESH)

    def ready():
        pl.semaphore_wait(barrier, ROWS + COLS - 2)
        for t in range(1, ROWS):
            pl.semaphore_signal(met_sem, inc=1, device_id=(lax.rem(r + t, ROWS), c), device_id_type=MESH)
        pl.semaphore_wait(met_sem, ROWS - 1)

    x, y, z = lax.div(c, 4), lax.rem(lax.div(c, 2), 2) * 2 + lax.div(r, 4), lax.rem(r, 4)

    def far_first(q):
        return 2 + q - lax.div(q, 2) * (2 * q - 1)

    def partner(t, g):
        dx = lax.rem(x + far_first(lax.rem(t, 4)), 4)
        dy = lax.rem(y + far_first(lax.rem(lax.div(t, 4), 4)), 4)
        dz = lax.rem(z + far_first(lax.div(t, 16)), 4)
        row = lax.rem(dy, 2) * 4 + dz
        col = dx * 4 + lax.div(dy, 2) * 2 + g
        d = row * COLS + col
        return d, g * PER + lax.div(d, 2), (row, col)

    def remote(src, dst, step, dev):
        pltpu.make_async_remote_copy(
            src_ref=src, dst_ref=dst, send_sem=send_sem.at[step],
            recv_sem=recv_sem.at[step], device_id=dev, device_id_type=MESH,
        ).start()

    def local(src, dst, step):
        pltpu.make_async_copy(src, dst, recv_sem.at[step]).start()

    def spread_channels(g, u):
        def one(t, _):
            d, ch, dev = partner(t, g)
            remote(send.at[ch], recv.at[u, me], 2 * u, dev)
            return 0

        lax.fori_loop(0, CHIPS - 1, one, 0)
        d, ch, dev = partner(CHIPS - 1, g)

        @pl.when(core == g)
        def _():
            local(send.at[ch], recv.at[u, me], 2 * u)

        @pl.when(core != g)
        def _():
            remote(send.at[ch], recv.at[u, me], 2 * u, dev)

    def spread_tri(g, u):
        def one(t, _):
            d, ch, dev = partner(t, g)
            remote(tri_send.at[d], tri_recv.at[u, mine], 2 * u + 1, dev)
            return 0

        lax.fori_loop(0, CHIPS - 1, one, 0)
        d, ch, dev = partner(CHIPS - 1, g)

        @pl.when(core == g)
        def _():
            local(tri_send.at[d], tri_recv.at[u, mine], 2 * u + 1)

        @pl.when(core != g)
        def _():
            remote(tri_send.at[d], tri_recv.at[u, mine], 2 * u + 1, dev)

    def arrived(dst, step):
        pltpu.make_async_copy(dst, dst, recv_sem.at[step]).wait()

    def left(src, step):
        rest = src.at[pl.ds(0, DEV - 1)]
        pltpu.make_async_copy(rest, rest, send_sem.at[step]).wait()

    def turn(u):
        whole = jnp.transpose(weight[u])
        for g in range(GROUPS):
            for k in range(4):
                wt[u, (4 * g + k) * PER : (4 * g + k + 1) * PER] = whole[k * CH + g * PER : k * CH + (g + 1) * PER]
        wt[u, 4 * CH :] = whole[4 * CH :]
        wot[u] = jnp.transpose(weight_out[u])
        for k in range(2):
            gcol[2 * u + k] = jnp.transpose(jnp.broadcast_to(gain[2 * u + k : 2 * u + k + 1, :], (CH, CH)))

    loads[0].wait()
    loads[1].wait()
    loads[3].wait()
    turn(0)
    loads[2].wait()
    for s in range(TILES):
        rows = jnp.concatenate([pair[pl.ds(p * TILES + s, A, stride=B), :] for p in range(2)], axis=0)
        turned = jnp.transpose(rows)
        state[:, s * CH : (s + 1) * CH] = turned
        normed[:, s * CH : (s + 1) * CH] = layer_norm(turned, gcol[0]).astype(jnp.bfloat16)

    for u in range(2):
        for g in range(GROUPS):
            w = wt[u, 4 * PER * g : 4 * PER * (g + 1)]

            def project(n, _):
                at = pl.ds(pl.multiple_of(n * WIDE, WIDE), WIDE)
                proj = dot(w, normed[:, at])
                le = sigmoid(proj[0:PER]) * proj[PER : 2 * PER]
                ri = sigmoid(proj[2 * PER : 3 * PER]) * proj[3 * PER : 4 * PER]
                for h in range(SUB):
                    s = n * SUB + h
                    wide[pl.ds(s, PER, stride=32), :] = le[:, h * CH : (h + 1) * CH]
                    wide[pl.ds(TILES + s, PER, stride=32), :] = ri[:, h * CH : (h + 1) * CH]
                return 0

            lax.fori_loop(0, STEPS, project, 0)
            if g == 0:
                if u == 0:
                    ready()
                else:
                    left(send, 0)

            def pack(n, _):
                send[pl.ds(g * PER + n * 16, 16)] = (
                    wide[pl.ds(pl.multiple_of(n * 512, 512), 512), :].astype(jnp.bfloat16).reshape(16, 32, CH)
                )
                return 0

            lax.fori_loop(0, PER // 16, pack, 0)
            spread_channels(g, u)

        def open_gate(n, _):
            at = pl.ds(pl.multiple_of(n * WIDE, WIDE), WIDE)
            gate[:, at] = sigmoid(dot(wt[u, 4 * CH :], normed[:, at]))
            return 0

        lax.fori_loop(0, STEPS, open_gate, 0)
        if u == 0:
            turn(1)
        arrived(recv.at[u], 2 * u)

        def join(cc, _):
            for rp in range(4):
                t0 = recv[u, 2 * rp * COLS + cc]
                t1 = recv[u, (2 * rp + 1) * COLS + cc]
                for x, lo in ((xl, 0), (xr, TILES)):
                    p0, p1 = swap_halves(t0[lo : lo + TILES], t1[lo : lo + TILES])
                    x[pl.ds(pl.multiple_of(cc * B, B), TILES), rp * CH : (rp + 1) * CH] = p0
                    x[pl.ds(pl.multiple_of(cc * B + TILES, TILES), TILES), rp * CH : (rp + 1) * CH] = p1
            return 0

        lax.fori_loop(0, COLS, join, 0)

        over = 0 if u == 0 else 1
        if u == 1:
            left(tri_send, 1)
        for h in range(4):
            if u == 0:
                lhs = xr[:, h * CH : (h + 1) * CH]
            else:
                lhs = xr[h * CH : (h + 1) * CH, :]
            tri = lax.dot_general(
                lhs, xl[...], (((over,), (over,)), ((), ())), preferred_element_type=jnp.float32
            ).astype(jnp.bfloat16)
            for i in range(4):
                cc = h * 4 + i
                for rp in range(4):
                    q0 = tri[i * B : i * B + TILES, rp * CH : (rp + 1) * CH]
                    q1 = tri[i * B + TILES : (i + 1) * B, rp * CH : (rp + 1) * CH]
                    p0, p1 = swap_halves(q0, q1)
                    tri_send[2 * rp * COLS + cc] = p0
                    tri_send[(2 * rp + 1) * COLS + cc] = p1
        for g in range(GROUPS):
            spread_tri(g, u)
        arrived(tri_recv.at[u], 2 * u + 1)

        def unpack(n, _):
            x = tri_recv[u, pl.ds(n * 16, 16)].astype(jnp.float32)
            wide[pl.ds(pl.multiple_of(n * 256, 256), 256), :] = x.reshape(16 * TILES, CH)
            return 0

        lax.fori_loop(0, CH // 16, unpack, 0)

        def finish(n, _):
            at = pl.ds(pl.multiple_of(n * WIDE, WIDE), WIDE)
            outnorm = [
                layer_norm(wide[pl.ds(n * SUB + h, CH, stride=TILES), :], gcol[2 * u + 1]).astype(jnp.bfloat16)
                for h in range(SUB)
            ]
            new = state[:, at] + gate[:, at] * dot(wot[u], jnp.concatenate(outnorm, axis=1))
            if u == 0:
                state[:, at] = new
            for h in range(SUB):
                part = new[:, h * CH : (h + 1) * CH]
                if u == 0:
                    normed[:, pl.ds(pl.multiple_of(n * WIDE + h * CH, CH), CH)] = layer_norm(part, gcol[2]).astype(jnp.bfloat16)
                else:
                    rows = jnp.transpose(part)
                    for p in range(2):
                        out[pl.ds(p * TILES + n * SUB + h, A, stride=B), :] = rows[p * A : (p + 1) * A]
            return 0

        lax.fori_loop(0, STEPS, finish, 0)
    left(send, 2)
    left(tri_send, 3)


def shards(pair, gain, weight, weight_out):
    hbm = pl.BlockSpec(memory_space=pltpu.HBM)
    f32, bf16 = jnp.float32, jnp.bfloat16
    result = pl.pallas_call(
        kernel,
        out_shape=jax.ShapeDtypeStruct((POS, CH), f32),
        in_specs=[hbm] * 4,
        out_specs=pl.BlockSpec(memory_space=pltpu.VMEM),
        scratch_shapes=[
            pltpu.VMEM((POS, CH), f32),
            pltpu.VMEM((4, CH), f32),
            pltpu.VMEM((2, CH, 5 * CH), bf16),
            pltpu.VMEM((2, CH, CH), bf16),
            pltpu.VMEM((CH, POS), f32),
            pltpu.VMEM((CH, POS), bf16),
            pltpu.VMEM((CH, POS), f32),
            pltpu.VMEM((2, 5 * CH, CH), bf16),
            pltpu.VMEM((2, CH, CH), bf16),
            pltpu.VMEM((4, CH, CH), f32),
            pltpu.VMEM((POS, CH), f32),
            pltpu.VMEM((DEV, 2 * TILES, CH), bf16),
            pltpu.VMEM((2, DEV, 2 * TILES, CH), bf16),
            pltpu.VMEM((N, N), bf16),
            pltpu.VMEM((N, N), bf16),
            pltpu.VMEM((DEV, TILES, CH), bf16),
            pltpu.VMEM((2, DEV, TILES, CH), bf16),
            pltpu.SemaphoreType.DMA((4,)),
            pltpu.SemaphoreType.DMA((4,)),
            pltpu.SemaphoreType.DMA((4,)),
            pltpu.SemaphoreType.REGULAR,
        ],
        compiler_params=pltpu.CompilerParams(
            collective_id=0, has_side_effects=True, vmem_limit_bytes=58 << 20
        ),
    )(pair.reshape(POS, CH), gain.reshape(4, CH), weight, weight_out)
    return result.reshape(A, B, CH)


def solution(mesh):
    placed = (P("row", "col", None), P(), P(), P())
    return jax.shard_map(
        shards, mesh=mesh, in_specs=placed, out_specs=P("row", "col", None), check_vma=False
    )
```

time: 79 us -> 70.2 us (0.89)
  Pallas kernels: 74 us -> 67.7 us
  local copies, waits for them, and re-layouts: 4.69 us -> 2.26 us
    pallas_call x1, Pallas kernels: 74 us -> 67.7 us  [shards(): pl.pallas_call(kernel, out_shape=jax.ShapeDtypeStruct((POS, CH), f32), in...]
    unnamed x9 -> x1, local copies, waits for them, and re-layouts: 4.69 us -> 2.26 us
where the time goes in v2:
time: 70.2 us; the launch traced here: 70 us
  Pallas kernels  67.7 us (96%)
  local copies, waits for them, and re-layouts  2.26 us (3%)
    pallas_call x1, Pallas kernels, shards(): pl.pallas_call(kernel, out_shape=jax.ShapeDtypeStruct((POS, CH), f32), in...  67.7 us
    unnamed x1, local copies, waits for them, and re-layouts  2.26 us

profile of v2, /device:TPU:1, one launch (start us, length us, event | category | flops | bytes accessed | tf_op | source)
XLA Modules:
  0.0 70.0 jit_solution(16499155917001140191)
XLA Ops:
  0.0 67.7 %shard_map.46 = f32[2048,128]{1,0:T(8,128)} custom-call(f32[2048,128]{1,0:T(8,128)} %bitcast.4, f32[4,128]{1,0:T(4,128)} %bitcast.5, bf16[2,128,640]{2,1,0:T(8,128)(2,1)} %weight_in.1, bf16[2,128,128]{2,1,0:T(8,128)(2,1)} %weight_out_in.1), custom_call_target="tpu_custom_call" | custom-call | tf_op jit(solution)/shard_map/pallas_call | solution.py:271
  67.8 2.3 %copy.6 = f32[64,32,128]{2,1,0:T(8,128)} copy(f32[64,32,128]{2,1,0:T(8,128)} %bitcast.3) | data formatting | bytes 2097152

commit v3 on v2

--- a/solution.py
+++ b/solution.py
@@ -5,7 +5,8 @@
 from jax.experimental.pallas import tpu as pltpu
 from jax.sharding import PartitionSpec as P
 
-MESH = pl.DeviceIdType.MESH
+LOGICAL = pl.DeviceIdType.LOGICAL
+FAR_FIRST = (2, 3, 1, 0)
 ROWS, COLS = 8, 16
 DEV = ROWS * COLS
 CHIPS = DEV // 2
@@ -18,6 +19,7 @@
 PER = CH // GROUPS
 WIDE = 512
 STEPS = POS // WIDE
+PLANE = DEV // 4
 SUB = WIDE // CH
 
 
@@ -46,7 +48,7 @@
 
 def kernel(pair_in, gain_in, weight_in, weight_out_in, out, pair, gain, weight, weight_out, state,
            normed, gate, wt, wot, gcol, wide, send, recv, xl, xr, tri_send, tri_recv, in_sem,
-           send_sem, recv_sem, met_sem):
+           send_sem, recv_sem):
     r, c = lax.axis_index("row"), lax.axis_index("col")
     me = r * COLS + c
     chip, core = lax.div(me, 2), lax.rem(me, 2)
@@ -61,77 +63,72 @@
     for load in loads:
         load.start()
 
+    x, y, z = lax.div(c, 4), lax.rem(lax.div(c, 2), 2) * 2 + lax.div(r, 4), lax.rem(r, 4)
+    along_x = [lax.rem(x + k, 4) * 2 for k in FAR_FIRST]
+    along_y = [lax.rem(lax.rem(y + k, 4), 2) * 32 + lax.div(lax.rem(y + k, 4), 2) for k in FAR_FIRST]
+    along_z = [lax.rem(z + k, 4) * 8 for k in FAR_FIRST]
+
+    def tour(visit):
+        for i in range(4):
+            def plane(j, _):
+                far = 2 + j - lax.div(j, 2) * (2 * j - 1)
+                at = along_x[i] + lax.rem(z + far, 4) * 8
+                for k in range(4):
+                    visit(at + along_y[k], i)
+                return 0
+
+            lax.fori_loop(0, 4 if i < 3 else 3, plane, 0)
+        for k in range(3):
+            visit(along_x[3] + along_z[3] + along_y[k], 3)
+
     barrier = pltpu.get_barrier_semaphore()
-    for t in range(1, ROWS):
-        pl.semaphore_signal(barrier, inc=1, device_id=(lax.rem(r + t, ROWS), c), device_id_type=MESH)
-    for t in range(1, COLS):
-        pl.semaphore_signal(barrier, inc=1, device_id=(r, lax.rem(c + t, COLS)), device_id_type=MESH)
+
+    def greet(g):
+        def visit(other, i):
+            pl.semaphore_signal(barrier, inc=1, device_id=other * 2 + g, device_id_type=LOGICAL)
+
+        tour(visit)
+
+    greet(0)
+    greet(1)
+    pl.semaphore_signal(barrier, inc=1, device_id=chip * 2 + 1 - core, device_id_type=LOGICAL)
 
     def ready():
-        pl.semaphore_wait(barrier, ROWS + COLS - 2)
-        for t in range(1, ROWS):
-            pl.semaphore_signal(met_sem, inc=1, device_id=(lax.rem(r + t, ROWS), c), device_id_type=MESH)
-        pl.semaphore_wait(met_sem, ROWS - 1)
-
-    x, y, z = lax.div(c, 4), lax.rem(lax.div(c, 2), 2) * 2 + lax.div(r, 4), lax.rem(r, 4)
-
-    def far_first(q):
-        return 2 + q - lax.div(q, 2) * (2 * q - 1)
-
-    def partner(t, g):
-        dx = lax.rem(x + far_first(lax.rem(t, 4)), 4)
-        dy = lax.rem(y + far_first(lax.rem(lax.div(t, 4), 4)), 4)
-        dz = lax.rem(z + far_first(lax.div(t, 16)), 4)
-        row = lax.rem(dy, 2) * 4 + dz
-        col = dx * 4 + lax.div(dy, 2) * 2 + g
-        d = row * COLS + col
-        return d, g * PER + lax.div(d, 2), (row, col)
-
-    def remote(src, dst, step, dev):
-        pltpu.make_async_remote_copy(
-            src_ref=src, dst_ref=dst, send_sem=send_sem.at[step],
-            recv_sem=recv_sem.at[step], device_id=dev, device_id_type=MESH,
-        ).start()
-
-    def local(src, dst, step):
-        pltpu.make_async_copy(src, dst, recv_sem.at[step]).start()
-
-    def spread_channels(g, u):
-        def one(t, _):
-            d, ch, dev = partner(t, g)
-            remote(send.at[ch], recv.at[u, me], 2 * u, dev)
-            return 0
-
-        lax.fori_loop(0, CHIPS - 1, one, 0)
-        d, ch, dev = partner(CHIPS - 1, g)
+        pl.semaphore_wait(barrier, DEV - 1)
+
+    def spread(src, dst, sends, recvs, g):
+        def visit(other, i):
+            pltpu.make_async_remote_copy(
+                src_ref=src(other), dst_ref=dst(i), send_sem=sends, recv_sem=recvs(i),
+                device_id=other * 2 + g, device_id_type=LOGICAL,
+            ).start()
+
+        tour(visit)
 
         @pl.when(core == g)
         def _():
-            local(send.at[ch], recv.at[u, me], 2 * u)
+            pltpu.make_async_copy(src(chip), dst(3), recvs(3)).start()
 
         @pl.when(core != g)
         def _():
-            remote(send.at[ch], recv.at[u, me], 2 * u, dev)
+            visit(chip, 3)
+
+    slot = r * 4 + lax.rem(c, 4)
+
+    def spread_channels(g, u):
+        spread(
+            lambda other: send.at[g * PER + other], lambda i: recv.at[u, i * PLANE + slot],
+            send_sem.at[2 * u], lambda i: recv_sem.at[u, i], g,
+        )
 
     def spread_tri(g, u):
-        def one(t, _):
-            d, ch, dev = partner(t, g)
-            remote(tri_send.at[d], tri_recv.at[u, mine], 2 * u + 1, dev)
-            return 0
-
-        lax.fori_loop(0, CHIPS - 1, one, 0)
-        d, ch, dev = partner(CHIPS - 1, g)
-
-        @pl.when(core == g)
-        def _():
-            local(tri_send.at[d], tri_recv.at[u, mine], 2 * u + 1)
-
-        @pl.when(core != g)
-        def _():
-            remote(tri_send.at[d], tri_recv.at[u, mine], 2 * u + 1, dev)
-
-    def arrived(dst, step):
-        pltpu.make_async_copy(dst, dst, recv_sem.at[step]).wait()
+        spread(
+            lambda other: tri_send.at[other * 2 + g], lambda i: tri_recv.at[u, mine],
+            send_sem.at[2 * u + 1], lambda i: recv_sem.at[u, 4], g,
+        )
+
+    def arrived(dst, sem):
+        pltpu.make_async_copy(dst, dst, sem).wait()
 
     def left(src, step):
         rest = src.at[pl.ds(0, DEV - 1)]
@@ -197,19 +194,22 @@
         lax.fori_loop(0, STEPS, open_gate, 0)
         if u == 0:
             turn(1)
-        arrived(recv.at[u], 2 * u)
-
-        def join(cc, _):
-            for rp in range(4):
-                t0 = recv[u, 2 * rp * COLS + cc]
-                t1 = recv[u, (2 * rp + 1) * COLS + cc]
-                for x, lo in ((xl, 0), (xr, TILES)):
-                    p0, p1 = swap_halves(t0[lo : lo + TILES], t1[lo : lo + TILES])
-                    x[pl.ds(pl.multiple_of(cc * B, B), TILES), rp * CH : (rp + 1) * CH] = p0
-                    x[pl.ds(pl.multiple_of(cc * B + TILES, TILES), TILES), rp * CH : (rp + 1) * CH] = p1
-            return 0
-
-        lax.fori_loop(0, COLS, join, 0)
+        for i, k in enumerate(FAR_FIRST):
+            arrived(recv.at[u, pl.ds(i * PLANE, PLANE)], recv_sem.at[u, i])
+            top = lax.rem(x + 4 - k, 4) * CH
+
+            def join(cc, _):
+                at = pl.multiple_of(top + cc * B, B)
+                for rp in range(4):
+                    t0 = recv[u, i * PLANE + 2 * rp * 4 + cc]
+                    t1 = recv[u, i * PLANE + (2 * rp + 1) * 4 + cc]
+                    for m, lo in ((xl, 0), (xr, TILES)):
+                        p0, p1 = swap_halves(t0[lo : lo + TILES], t1[lo : lo + TILES])
+                        m[pl.ds(at, TILES), rp * CH : (rp + 1) * CH] = p0
+                        m[pl.ds(pl.multiple_of(at + TILES, TILES), TILES), rp * CH : (rp + 1) * CH] = p1
+                return 0
+
+            lax.fori_loop(0, 4, join, 0)
 
         over = 0 if u == 0 else 1
         if u == 1:
@@ -232,7 +232,7 @@
                     tri_send[(2 * rp + 1) * COLS + cc] = p1
         for g in range(GROUPS):
             spread_tri(g, u)
-        arrived(tri_recv.at[u], 2 * u + 1)
+        arrived(tri_recv.at[u], recv_sem.at[u, 4])
 
         def unpack(n, _):
             x = tri_recv[u, pl.ds(n * 16, 16)].astype(jnp.float32)
@@ -293,13 +293,12 @@
             pltpu.VMEM((2, DEV, TILES, CH), bf16),
             pltpu.SemaphoreType.DMA((4,)),
             pltpu.SemaphoreType.DMA((4,)),
-            pltpu.SemaphoreType.DMA((4,)),
-            pltpu.SemaphoreType.REGULAR,
+            pltpu.SemaphoreType.DMA((2, 5)),
         ],
         compiler_params=pltpu.CompilerParams(
-            collective_id=0, has_side_effects=True, vmem_limit_bytes=58 << 20
+            collective_id=0, has_side_effects=True, vmem_limit_bytes=40 << 20
         ),
-    )(pair.reshape(POS, CH), gain.reshape(4, CH), weight, weight_out)
+    )(*[pltpu.with_memory_space_constraint(v, pltpu.HBM) for v in (pair.reshape(POS, CH), gain.reshape(4, CH), weight, weight_out)])
     return result.reshape(A, B, CH)
 
 

time: 70.2 us -> 63.3 us (0.902)
  Pallas kernels: 67.7 us -> 62.2 us
  local copies, waits for them, and re-layouts: 2.26 us -> 0.97 us
    pallas_call x1, Pallas kernels: 67.7 us -> 62.2 us  [shards(): pl.pallas_call(kernel, out_shape=jax.ShapeDtypeStruct((POS, CH), f32), in...]
    unnamed x1, local copies, waits for them, and re-layouts: 2.26 us -> 0.97 us
where the time goes in v3:
time: 63.3 us; the launch traced here: 63.2 us
  Pallas kernels  62.2 us (98%)
  local copies, waits for them, and re-layouts  0.97 us (2%)
    pallas_call x1, Pallas kernels, shards(): pl.pallas_call(kernel, out_shape=jax.ShapeDtypeStruct((POS, CH), f32), in...  62.2 us

profile of v3, /device:TPU:1, one launch (start us, length us, event | category | flops | bytes accessed | tf_op | source)
XLA Modules:
  0.0 63.2 jit_solution(16074098019598430837)
XLA Ops:
  0.0 62.2 %shard_map.46 = f32[2048,128]{1,0:T(8,128)S(1)} custom-call(f32[2048,128]{1,0:T(8,128)} %bitcast.4, f32[4,128]{1,0:T(4,128)} %bitcast.5, bf16[2,128,640]{2,1,0:T(8,128)(2,1)} %weight_in.1, bf16[2,128,128]{2,1,0:T(8,128)(2,1)} %weight_out_in.1), custom_call_target="tpu_custom_call" | custom-call | tf_op jit(solution)/shard_map/pallas_call | solution.py:271
  62.2 1.0 %copy.6 = f32[64,32,128]{2,1,0:T(8,128)} copy(f32[64,32,128]{2,1,0:T(8,128)S(1)} %bitcast.3) | data formatting | bytes 2097152

commit v4 on v3

--- a/solution.py
+++ b/solution.py
@@ -15,8 +15,7 @@
 POS = A * B
 TILES = 16
 N = 512
-GROUPS = 2
-PER = CH // GROUPS
+PER = 16
 WIDE = 512
 STEPS = POS // WIDE
 PLANE = DEV // 4
@@ -47,12 +46,11 @@
 
 
 def kernel(pair_in, gain_in, weight_in, weight_out_in, out, pair, gain, weight, weight_out, state,
-           normed, gate, wt, wot, gcol, wide, send, recv, xl, xr, tri_send, tri_recv, in_sem,
+           normed, gate, wt, wot, gcol, wide, send, recv, xl, xr, turned, tri_send, tri_recv, in_sem,
            send_sem, recv_sem):
     r, c = lax.axis_index("row"), lax.axis_index("col")
     me = r * COLS + c
     chip, core = lax.div(me, 2), lax.rem(me, 2)
-    mine = core * PER + chip
 
     loads = [
         pltpu.make_async_copy(x, y, in_sem.at[i])
@@ -64,30 +62,38 @@
         load.start()
 
     x, y, z = lax.div(c, 4), lax.rem(lax.div(c, 2), 2) * 2 + lax.div(r, 4), lax.rem(r, 4)
-    along_x = [lax.rem(x + k, 4) * 2 for k in FAR_FIRST]
-    along_y = [lax.rem(lax.rem(y + k, 4), 2) * 32 + lax.div(lax.rem(y + k, 4), 2) for k in FAR_FIRST]
-    along_z = [lax.rem(z + k, 4) * 8 for k in FAR_FIRST]
-
-    def tour(visit):
+    mine = (core * 4 + x) * PER + r * 2 + lax.div(y, 2)
+
+    def in_y(k):
+        at = lax.rem(y + k, 4)
+        lo, hi = lax.rem(at, 2), lax.div(at, 2)
+        return lo * 32 + hi, lo * 8 + hi
+
+    along_x = [lax.rem(x + k, 4) for k in FAR_FIRST]
+    along_y = [in_y(k) for k in FAR_FIRST]
+
+    def tour(i, visit):
+        def stop(far, ks):
+            at = lax.rem(z + far, 4)
+            for k in ks:
+                visit(along_x[i] * 2 + at * 8 + along_y[k][0], at * 2 + along_y[k][1])
+
+        def plane(j, _):
+            stop(2 + j - lax.div(j, 2) * (2 * j - 1), range(4))
+            return 0
+
+        lax.fori_loop(0, 4 if i < 3 else 3, plane, 0)
+        if i == 3:
+            stop(0, range(3))
+
+    barrier = pltpu.get_barrier_semaphore()
+
+    def greet(g):
+        def visit(other, place):
+            pl.semaphore_signal(barrier, inc=1, device_id=other * 2 + g, device_id_type=LOGICAL)
+
         for i in range(4):
-            def plane(j, _):
-                far = 2 + j - lax.div(j, 2) * (2 * j - 1)
-                at = along_x[i] + lax.rem(z + far, 4) * 8
-                for k in range(4):
-                    visit(at + along_y[k], i)
-                return 0
-
-            lax.fori_loop(0, 4 if i < 3 else 3, plane, 0)
-        for k in range(3):
-            visit(along_x[3] + along_z[3] + along_y[k], 3)
-
-    barrier = pltpu.get_barrier_semaphore()
-
-    def greet(g):
-        def visit(other, i):
-            pl.semaphore_signal(barrier, inc=1, device_id=other * 2 + g, device_id_type=LOGICAL)
-
-        tour(visit)
+            tour(i, visit)
 
     greet(0)
     greet(1)
@@ -96,35 +102,37 @@
     def ready():
         pl.semaphore_wait(barrier, DEV - 1)
 
-    def spread(src, dst, sends, recvs, g):
-        def visit(other, i):
+    def spread(src, dst, sends, recvs, g, i):
+        def visit(other, place):
             pltpu.make_async_remote_copy(
-                src_ref=src(other), dst_ref=dst(i), send_sem=sends, recv_sem=recvs(i),
+                src_ref=src(other, place), dst_ref=dst, send_sem=sends, recv_sem=recvs,
                 device_id=other * 2 + g, device_id_type=LOGICAL,
             ).start()
 
-        tour(visit)
-
-        @pl.when(core == g)
-        def _():
-            pltpu.make_async_copy(src(chip), dst(3), recvs(3)).start()
-
-        @pl.when(core != g)
-        def _():
-            visit(chip, 3)
+        tour(i, visit)
+        if i == 3:
+            place = r * 2 + lax.div(y, 2)
+
+            @pl.when(core == g)
+            def _():
+                pltpu.make_async_copy(src(chip, place), dst, recvs).start()
+
+            @pl.when(core != g)
+            def _():
+                visit(chip, place)
 
     slot = r * 4 + lax.rem(c, 4)
 
-    def spread_channels(g, u):
+    def spread_channels(g, i, u):
         spread(
-            lambda other: send.at[g * PER + other], lambda i: recv.at[u, i * PLANE + slot],
-            send_sem.at[2 * u], lambda i: recv_sem.at[u, i], g,
+            lambda other, place: send.at[(g * 4 + i) * PER + place], recv.at[u, i * PLANE + slot],
+            send_sem.at[2 * u], recv_sem.at[u, i], g, i,
         )
 
-    def spread_tri(g, u):
+    def spread_tri(g, i, u):
         spread(
-            lambda other: tri_send.at[other * 2 + g], lambda i: tri_recv.at[u, mine],
-            send_sem.at[2 * u + 1], lambda i: recv_sem.at[u, 4], g,
+            lambda other, place: tri_send.at[other * 2 + g], tri_recv.at[u, mine],
+            send_sem.at[2 * u + 1], recv_sem.at[u, 4], g, i,
         )
 
     def arrived(dst, sem):
@@ -136,9 +144,9 @@
 
     def turn(u):
         whole = jnp.transpose(weight[u])
-        for g in range(GROUPS):
+        for n in range(CH // PER):
             for k in range(4):
-                wt[u, (4 * g + k) * PER : (4 * g + k + 1) * PER] = whole[k * CH + g * PER : k * CH + (g + 1) * PER]
+                wt[u, (4 * n + k) * PER : (4 * n + k + 1) * PER] = whole[k * CH + n * PER : k * CH + (n + 1) * PER]
         wt[u, 4 * CH :] = whole[4 * CH :]
         wot[u] = jnp.transpose(weight_out[u])
         for k in range(2):
@@ -151,47 +159,47 @@
     loads[2].wait()
     for s in range(TILES):
         rows = jnp.concatenate([pair[pl.ds(p * TILES + s, A, stride=B), :] for p in range(2)], axis=0)
-        turned = jnp.transpose(rows)
-        state[:, s * CH : (s + 1) * CH] = turned
-        normed[:, s * CH : (s + 1) * CH] = layer_norm(turned, gcol[0]).astype(jnp.bfloat16)
+        values = jnp.transpose(rows)
+        state[:, s * CH : (s + 1) * CH] = values
+        normed[:, s * CH : (s + 1) * CH] = layer_norm(values, gcol[0]).astype(jnp.bfloat16)
 
     for u in range(2):
-        for g in range(GROUPS):
-            w = wt[u, 4 * PER * g : 4 * PER * (g + 1)]
-
-            def project(n, _):
-                at = pl.ds(pl.multiple_of(n * WIDE, WIDE), WIDE)
-                proj = dot(w, normed[:, at])
-                le = sigmoid(proj[0:PER]) * proj[PER : 2 * PER]
-                ri = sigmoid(proj[2 * PER : 3 * PER]) * proj[3 * PER : 4 * PER]
-                for h in range(SUB):
-                    s = n * SUB + h
-                    wide[pl.ds(s, PER, stride=32), :] = le[:, h * CH : (h + 1) * CH]
-                    wide[pl.ds(TILES + s, PER, stride=32), :] = ri[:, h * CH : (h + 1) * CH]
-                return 0
-
-            lax.fori_loop(0, STEPS, project, 0)
-            if g == 0:
+        for n in range(4):
+            g, first = n // 2, n % 2 * 2
+            w = jnp.concatenate(
+                [
+                    wt[u, pl.ds(pl.multiple_of((g * 4 + along_x[i]) * 4 * PER, 4 * PER), 4 * PER), :]
+                    for i in (first, first + 1)
+                ],
+                axis=0,
+            )
+            base = n % 2 * (POS // 2)
+            for m in range(STEPS):
+                proj = dot(w, normed[:, m * WIDE : (m + 1) * WIDE])
+                for e in range(2):
+                    part = [proj[(4 * e + k) * PER : (4 * e + k + 1) * PER] for k in range(4)]
+                    both = (sigmoid(part[0]) * part[1], sigmoid(part[2]) * part[3])
+                    for h in range(SUB):
+                        for k in range(2):
+                            wide[pl.ds(base + e * 32 * PER + k * TILES + m * SUB + h, PER, stride=32), :] = (
+                                both[k][:, h * CH : (h + 1) * CH]
+                            )
+            if n == 0:
                 if u == 0:
                     ready()
                 else:
                     left(send, 0)
-
-            def pack(n, _):
-                send[pl.ds(g * PER + n * 16, 16)] = (
-                    wide[pl.ds(pl.multiple_of(n * 512, 512), 512), :].astype(jnp.bfloat16).reshape(16, 32, CH)
-                )
-                return 0
-
-            lax.fori_loop(0, PER // 16, pack, 0)
-            spread_channels(g, u)
+            for i in (first, first + 1):
+                rows = wide[pl.ds(base + (i - first) * 32 * PER, 32 * PER), :]
+                send[(g * 4 + i) * PER : (g * 4 + i + 1) * PER] = rows.astype(jnp.bfloat16).reshape(PER, 32, CH)
+                spread_channels(g, i, u)
 
         def open_gate(n, _):
             at = pl.ds(pl.multiple_of(n * WIDE, WIDE), WIDE)
             gate[:, at] = sigmoid(dot(wt[u, 4 * CH :], normed[:, at]))
             return 0
 
-        lax.fori_loop(0, STEPS, open_gate, 0)
+        lax.fori_loop(0, STEPS, open_gate, 0, unroll=True)
         if u == 0:
             turn(1)
         for i, k in enumerate(FAR_FIRST):
@@ -209,19 +217,18 @@
                         m[pl.ds(pl.multiple_of(at + TILES, TILES), TILES), rp * CH : (rp + 1) * CH] = p1
                 return 0
 
-            lax.fori_loop(0, 4, join, 0)
-
-        over = 0 if u == 0 else 1
+            lax.fori_loop(0, 4, join, 0, unroll=True)
+            block = pl.ds(pl.multiple_of(top, CH), CH)
+            turned[:, block] = jnp.transpose((xr if u == 0 else xl)[block, :])
+
         if u == 1:
             left(tri_send, 1)
         for h in range(4):
+            rows = pl.ds(h * CH, CH)
             if u == 0:
-                lhs = xr[:, h * CH : (h + 1) * CH]
+                tri = dot(turned[rows, :], xl[...]).astype(jnp.bfloat16)
             else:
-                lhs = xr[h * CH : (h + 1) * CH, :]
-            tri = lax.dot_general(
-                lhs, xl[...], (((over,), (over,)), ((), ())), preferred_element_type=jnp.float32
-            ).astype(jnp.bfloat16)
+                tri = dot(xr[rows, :], turned[...]).astype(jnp.bfloat16)
             for i in range(4):
                 cc = h * 4 + i
                 for rp in range(4):
@@ -230,8 +237,9 @@
                     p0, p1 = swap_halves(q0, q1)
                     tri_send[2 * rp * COLS + cc] = p0
                     tri_send[(2 * rp + 1) * COLS + cc] = p1
-        for g in range(GROUPS):
-            spread_tri(g, u)
+        for g in (0, 1) if u == 0 else (1, 0):
+            for i in range(4):
+                spread_tri(g, i, u)
         arrived(tri_recv.at[u], recv_sem.at[u, 4])
 
         def unpack(n, _):
@@ -260,7 +268,7 @@
                         out[pl.ds(p * TILES + n * SUB + h, A, stride=B), :] = rows[p * A : (p + 1) * A]
             return 0
 
-        lax.fori_loop(0, STEPS, finish, 0)
+        lax.fori_loop(0, STEPS, finish, 0, unroll=True)
     left(send, 2)
     left(tri_send, 3)
 
@@ -289,6 +297,7 @@
             pltpu.VMEM((2, DEV, 2 * TILES, CH), bf16),
             pltpu.VMEM((N, N), bf16),
             pltpu.VMEM((N, N), bf16),
+            pltpu.VMEM((N, N), bf16),
             pltpu.VMEM((DEV, TILES, CH), bf16),
             pltpu.VMEM((2, DEV, TILES, CH), bf16),
             pltpu.SemaphoreType.DMA((4,)),

time: 63.3 us -> 61.7 us (0.975); the launches traced: 63.2 us -> 60.6 us
  Pallas kernels: 62.2 us -> 59.7 us
    pallas_call x1, Pallas kernels: 62.2 us -> 59.7 us  [shards(): pl.pallas_call(kernel, out_shape=jax.ShapeDtypeStruct((POS, CH), f32), in...]
where the time goes in v4:
time: 61.7 us; the launch traced here: 60.6 us
  Pallas kernels  59.7 us (97%)
  local copies, waits for them, and re-layouts  0.97 us (2%)
    pallas_call x1, Pallas kernels, shards(): pl.pallas_call(kernel, out_shape=jax.ShapeDtypeStruct((POS, CH), f32), in...  59.7 us

profile of v4, /device:TPU:1, one launch (start us, length us, event | category | flops | bytes accessed | tf_op | source)
XLA Modules:
  0.0 60.6 jit_solution(10162760447131152206)
XLA Ops:
  0.0 59.7 %shard_map.46 = f32[2048,128]{1,0:T(8,128)S(1)} custom-call(f32[2048,128]{1,0:T(8,128)} %bitcast.4, f32[4,128]{1,0:T(4,128)} %bitcast.5, bf16[2,128,640]{2,1,0:T(8,128)(2,1)} %weight_in.1, bf16[2,128,128]{2,1,0:T(8,128)(2,1)} %weight_out_in.1), custom_call_target="tpu_custom_call" | custom-call | tf_op jit(solution)/shard_map/pallas_call | solution.py:279
  59.7 1.0 %copy.6 = f32[64,32,128]{2,1,0:T(8,128)} copy(f32[64,32,128]{2,1,0:T(8,128)S(1)} %bitcast.3) | data formatting | bytes 2097152

commit v5 on v4

--- a/solution.py
+++ b/solution.py
@@ -18,6 +18,8 @@
 PER = 16
 WIDE = 512
 STEPS = POS // WIDE
+APART = 40
+CLOSE = 24
 PLANE = DEV // 4
 SUB = WIDE // CH
 
@@ -173,7 +175,7 @@
                 ],
                 axis=0,
             )
-            base = n % 2 * (POS // 2)
+            base = n % 2 * 2 * PER * APART
             for m in range(STEPS):
                 proj = dot(w, normed[:, m * WIDE : (m + 1) * WIDE])
                 for e in range(2):
@@ -181,18 +183,20 @@
                     both = (sigmoid(part[0]) * part[1], sigmoid(part[2]) * part[3])
                     for h in range(SUB):
                         for k in range(2):
-                            wide[pl.ds(base + e * 32 * PER + k * TILES + m * SUB + h, PER, stride=32), :] = (
+                            wide[pl.ds(base + e * APART * PER + k * TILES + m * SUB + h, PER, stride=APART), :] = (
                                 both[k][:, h * CH : (h + 1) * CH]
                             )
-            if n == 0:
-                if u == 0:
-                    ready()
-                else:
-                    left(send, 0)
+            if n == 0 and u == 1:
+                left(send, 0)
             for i in (first, first + 1):
-                rows = wide[pl.ds(base + (i - first) * 32 * PER, 32 * PER), :]
-                send[(g * 4 + i) * PER : (g * 4 + i + 1) * PER] = rows.astype(jnp.bfloat16).reshape(PER, 32, CH)
-                spread_channels(g, i, u)
+                for k in range(PER):
+                    rows = wide[pl.ds(base + ((i - first) * PER + k) * APART, 2 * TILES), :]
+                    send[(g * 4 + i) * PER + k] = rows.astype(jnp.bfloat16)
+            if n == 1 and u == 0:
+                ready()
+            if n % 2 == 1:
+                for i in range(4):
+                    spread_channels(g, i, u)
 
         def open_gate(n, _):
             at = pl.ds(pl.multiple_of(n * WIDE, WIDE), WIDE)
@@ -243,8 +247,9 @@
         arrived(tri_recv.at[u], recv_sem.at[u, 4])
 
         def unpack(n, _):
-            x = tri_recv[u, pl.ds(n * 16, 16)].astype(jnp.float32)
-            wide[pl.ds(pl.multiple_of(n * 256, 256), 256), :] = x.reshape(16 * TILES, CH)
+            for k in range(16):
+                at = pl.multiple_of((n * 16 + k) * CLOSE, 8)
+                wide[pl.ds(at, TILES), :] = tri_recv[u, n * 16 + k].astype(jnp.float32)
             return 0
 
         lax.fori_loop(0, CH // 16, unpack, 0)
@@ -252,7 +257,7 @@
         def finish(n, _):
             at = pl.ds(pl.multiple_of(n * WIDE, WIDE), WIDE)
             outnorm = [
-                layer_norm(wide[pl.ds(n * SUB + h, CH, stride=TILES), :], gcol[2 * u + 1]).astype(jnp.bfloat16)
+                layer_norm(wide[pl.ds(n * SUB + h, CH, stride=CLOSE), :], gcol[2 * u + 1]).astype(jnp.bfloat16)
                 for h in range(SUB)
             ]
             new = state[:, at] + gate[:, at] * dot(wot[u], jnp.concatenate(outnorm, axis=1))
@@ -292,7 +297,7 @@
             pltpu.VMEM((2, 5 * CH, CH), bf16),
             pltpu.VMEM((2, CH, CH), bf16),
             pltpu.VMEM((4, CH, CH), f32),
-            pltpu.VMEM((POS, CH), f32),
+            pltpu.VMEM((CLOSE * CH, CH), f32),
             pltpu.VMEM((DEV, 2 * TILES, CH), bf16),
             pltpu.VMEM((2, DEV, 2 * TILES, CH), bf16),
             pltpu.VMEM((N, N), bf16),

time: 61.7 us -> 58.6 us (0.950)
  Pallas kernels: 59.7 us -> 57 us
    pallas_call x1, Pallas kernels: 59.7 us -> 57 us  [shards(): pl.pallas_call(kernel, out_shape=jax.ShapeDtypeStruct((POS, CH), f32), in...]
where the time goes in v5:
time: 58.6 us; the launch traced here: 58 us
  Pallas kernels  57 us (97%)
  local copies, waits for them, and re-layouts  0.97 us (2%)
    pallas_call x1, Pallas kernels, shards(): pl.pallas_call(kernel, out_shape=jax.ShapeDtypeStruct((POS, CH), f32), in...  57 us

profile of v5, /device:TPU:1, one launch (start us, length us, event | category | flops | bytes accessed | tf_op | source)
XLA Modules:
  0.0 58.0 jit_solution(15413510655554369357)
XLA Ops:
  0.0 57.0 %shard_map.46 = f32[2048,128]{1,0:T(8,128)S(1)} custom-call(f32[2048,128]{1,0:T(8,128)} %bitcast.4, f32[4,128]{1,0:T(4,128)} %bitcast.5, bf16[2,128,640]{2,1,0:T(8,128)(2,1)} %weight_in.1, bf16[2,128,128]{2,1,0:T(8,128)(2,1)} %weight_out_in.1), custom_call_target="tpu_custom_call" | custom-call | tf_op jit(solution)/shard_map/pallas_call | solution.py:284
  57.0 1.0 %copy.6 = f32[64,32,128]{2,1,0:T(8,128)} copy(f32[64,32,128]{2,1,0:T(8,128)S(1)} %bitcast.3) | data formatting | bytes 2097152

commit v6 on v5

--- a/solution.py
+++ b/solution.py
@@ -43,12 +43,20 @@
     )
 
 
+def join_tiles(read, to, at):
+    for k in range(4):
+        lanes = pl.ds(k * CH, CH)
+        p0, p1 = swap_halves(read(2 * k), read(2 * k + 1))
+        to[pl.ds(at, TILES), lanes] = p0
+        to[pl.ds(pl.multiple_of(at + TILES, TILES), TILES), lanes] = p1
+
+
 def dot(a, b):
     return jnp.dot(a, b, preferred_element_type=jnp.float32)
 
 
 def kernel(pair_in, gain_in, weight_in, weight_out_in, out, pair, gain, weight, weight_out, state,
-           normed, gate, wt, wot, gcol, wide, send, recv, xl, xr, turned, tri_send, tri_recv, in_sem,
+           normed, gate, wt, wot, gcol, wide, send_a, send_b, send, recv_a, recv_b, recv, xl, xr, xf, turned, tri_send, tri_recv, in_sem,
            send_sem, recv_sem):
     r, c = lax.axis_index("row"), lax.axis_index("col")
     me = r * COLS + c
@@ -126,9 +134,16 @@
     slot = r * 4 + lax.rem(c, 4)
 
     def spread_channels(g, i, u):
+        src, dst = (send_a, recv_a) if u == 0 else (send, recv)
         spread(
-            lambda other, place: send.at[(g * 4 + i) * PER + place], recv.at[u, i * PLANE + slot],
+            lambda other, place: src.at[(g * 4 + i) * PER + place], dst.at[i * PLANE + slot],
             send_sem.at[2 * u], recv_sem.at[u, i], g, i,
+        )
+
+    def spread_late(g, i):
+        spread(
+            lambda other, place: send_b.at[(g * 4 + i) * PER + place], recv_b.at[i * PLANE + slot],
+            send_sem.at[4], recv_sem.at[2, i], g, i,
         )
 
     def spread_tri(g, i, u):
@@ -166,6 +181,7 @@
         normed[:, s * CH : (s + 1) * CH] = layer_norm(values, gcol[0]).astype(jnp.bfloat16)
 
     for u in range(2):
+        low = lax.rem(lax.broadcasted_iota(jnp.int32, (8, CH), 1), 2 * B) < B
         for n in range(4):
             g, first = n // 2, n % 2 * 2
             w = jnp.concatenate(
@@ -186,17 +202,28 @@
                             wide[pl.ds(base + e * APART * PER + k * TILES + m * SUB + h, PER, stride=APART), :] = (
                                 both[k][:, h * CH : (h + 1) * CH]
                             )
-            if n == 0 and u == 1:
-                left(send, 0)
             for i in (first, first + 1):
                 for k in range(PER):
-                    rows = wide[pl.ds(base + ((i - first) * PER + k) * APART, 2 * TILES), :]
-                    send[(g * 4 + i) * PER + k] = rows.astype(jnp.bfloat16)
+                    start = base + ((i - first) * PER + k) * APART
+                    at = (g * 4 + i) * PER + k
+                    if u == 1:
+                        send[at] = wide[pl.ds(start, 2 * TILES), :].astype(jnp.bfloat16)
+                    else:
+                        s0 = wide[pl.ds(start + TILES, 8), :]
+                        s1 = wide[pl.ds(start + TILES + 8, 8), :]
+                        first_half = jnp.where(low, s0, pltpu.roll(s1, B, 1))
+                        second_half = jnp.where(low, pltpu.roll(s0, CH - B, 1), s1)
+                        both = jnp.concatenate([wide[pl.ds(start, TILES), :], first_half], axis=0)
+                        send_a[at] = both.astype(jnp.bfloat16)
+                        send_b[at] = second_half.astype(jnp.bfloat16)
             if n == 1 and u == 0:
                 ready()
             if n % 2 == 1:
                 for i in range(4):
                     spread_channels(g, i, u)
+        if u == 0:
+            for n in range(8):
+                spread_late(n // 4, n % 4)
 
         def open_gate(n, _):
             at = pl.ds(pl.multiple_of(n * WIDE, WIDE), WIDE)
@@ -206,44 +233,73 @@
         lax.fori_loop(0, STEPS, open_gate, 0, unroll=True)
         if u == 0:
             turn(1)
-        for i, k in enumerate(FAR_FIRST):
-            arrived(recv.at[u, pl.ds(i * PLANE, PLANE)], recv_sem.at[u, i])
-            top = lax.rem(x + 4 - k, 4) * CH
-
-            def join(cc, _):
-                at = pl.multiple_of(top + cc * B, B)
-                for rp in range(4):
-                    t0 = recv[u, i * PLANE + 2 * rp * 4 + cc]
-                    t1 = recv[u, i * PLANE + (2 * rp + 1) * 4 + cc]
-                    for m, lo in ((xl, 0), (xr, TILES)):
-                        p0, p1 = swap_halves(t0[lo : lo + TILES], t1[lo : lo + TILES])
-                        m[pl.ds(at, TILES), rp * CH : (rp + 1) * CH] = p0
-                        m[pl.ds(pl.multiple_of(at + TILES, TILES), TILES), rp * CH : (rp + 1) * CH] = p1
-                return 0
-
-            lax.fori_loop(0, 4, join, 0, unroll=True)
-            block = pl.ds(pl.multiple_of(top, CH), CH)
-            turned[:, block] = jnp.transpose((xr if u == 0 else xl)[block, :])
+        def join_half(src, i, cc, lo, top):
+            for m in range(2):
+                v = [src[i * PLANE + (4 * m + q) * 4 + cc, pl.ds(lo, 8), :].astype(jnp.float32) for q in range(4)]
+                for k in range(4):
+                    at = pl.multiple_of(top + cc * B + k * 8, 8)
+                    xf[pl.ds(at, 8), m * CH : (m + 1) * CH] = jnp.concatenate(
+                        [piece[:, k * B : (k + 1) * B] for piece in v], axis=1
+                    )
+
+        def send_half(half):
+            for h in range(2):
+                tri = dot(turned[pl.ds(h * CH, CH), :], xl[...]).astype(jnp.bfloat16)
+                for q in range(4):
+                    cc = 2 * (4 * h + q) + half
+                    for rp in range(4):
+                        q0 = tri[q * B : q * B + TILES, rp * CH : (rp + 1) * CH]
+                        q1 = tri[q * B + TILES : (q + 1) * B, rp * CH : (rp + 1) * CH]
+                        p0, p1 = swap_halves(q0, q1)
+                        tri_send[2 * rp * COLS + cc] = p0
+                        tri_send[(2 * rp + 1) * COLS + cc] = p1
+            for i in range(4):
+                spread_tri(half, i, u)
+
+        for half in range(2 - u):
+            for i, k in enumerate(FAR_FIRST):
+                top = lax.rem(x + 4 - k, 4) * CH
+                block = pl.ds(pl.multiple_of(top, CH), CH)
+                plane = pl.ds(i * PLANE, PLANE)
+                if u == 1:
+                    arrived(recv.at[plane], recv_sem.at[1, i])
+                elif half == 0:
+                    arrived(recv_a.at[plane], recv_sem.at[0, i])
+                else:
+                    arrived(recv_b.at[plane], recv_sem.at[2, i])
+                for cc in range(4):
+                    at = pl.multiple_of(top + cc * B, B)
+                    place = lambda row: i * PLANE + row * 4 + cc
+                    if u == 1:
+                        join_tiles(lambda row: recv[place(row), pl.ds(0, TILES), :], xl, at)
+                        join_tiles(lambda row: recv[place(row), pl.ds(TILES, TILES), :], xr, at)
+                    elif half == 0:
+                        join_tiles(lambda row: recv_a[place(row), pl.ds(0, TILES), :], xl, at)
+                        join_half(recv_a, i, cc, TILES, top)
+                    else:
+                        join_half(recv_b, i, cc, 0, top)
+                if u == 1:
+                    turned[:, block] = jnp.transpose(xl[block, :])
+                else:
+                    turned[0 : N // 2, block] = jnp.transpose(xf[block, :].astype(jnp.bfloat16))
+            if u == 0:
+                send_half(half)
 
         if u == 1:
             left(tri_send, 1)
-        for h in range(4):
-            rows = pl.ds(h * CH, CH)
-            if u == 0:
-                tri = dot(turned[rows, :], xl[...]).astype(jnp.bfloat16)
-            else:
-                tri = dot(xr[rows, :], turned[...]).astype(jnp.bfloat16)
-            for i in range(4):
-                cc = h * 4 + i
-                for rp in range(4):
-                    q0 = tri[i * B : i * B + TILES, rp * CH : (rp + 1) * CH]
-                    q1 = tri[i * B + TILES : (i + 1) * B, rp * CH : (rp + 1) * CH]
-                    p0, p1 = swap_halves(q0, q1)
-                    tri_send[2 * rp * COLS + cc] = p0
-                    tri_send[(2 * rp + 1) * COLS + cc] = p1
-        for g in (0, 1) if u == 0 else (1, 0):
-            for i in range(4):
-                spread_tri(g, i, u)
+            for h in range(4):
+                tri = dot(xr[pl.ds(h * CH, CH), :], turned[...]).astype(jnp.bfloat16)
+                for i in range(4):
+                    cc = h * 4 + i
+                    for rp in range(4):
+                        q0 = tri[i * B : i * B + TILES, rp * CH : (rp + 1) * CH]
+                        q1 = tri[i * B + TILES : (i + 1) * B, rp * CH : (rp + 1) * CH]
+                        p0, p1 = swap_halves(q0, q1)
+                        tri_send[2 * rp * COLS + cc] = p0
+                        tri_send[(2 * rp + 1) * COLS + cc] = p1
+            for g in (1, 0):
+                for i in range(4):
+                    spread_tri(g, i, u)
         arrived(tri_recv.at[u], recv_sem.at[u, 4])
 
         def unpack(n, _):
@@ -274,6 +330,8 @@
             return 0
 
         lax.fori_loop(0, STEPS, finish, 0, unroll=True)
+    left(send_a, 0)
+    left(send_b, 4)
     left(send, 2)
     left(tri_send, 3)
 
@@ -298,16 +356,21 @@
             pltpu.VMEM((2, CH, CH), bf16),
             pltpu.VMEM((4, CH, CH), f32),
             pltpu.VMEM((CLOSE * CH, CH), f32),
+            pltpu.VMEM((DEV, TILES + 8, CH), bf16),
+            pltpu.VMEM((DEV, 8, CH), bf16),
             pltpu.VMEM((DEV, 2 * TILES, CH), bf16),
-            pltpu.VMEM((2, DEV, 2 * TILES, CH), bf16),
+            pltpu.VMEM((DEV, TILES + 8, CH), bf16),
+            pltpu.VMEM((DEV, 8, CH), bf16),
+            pltpu.VMEM((DEV, 2 * TILES, CH), bf16),
             pltpu.VMEM((N, N), bf16),
             pltpu.VMEM((N, N), bf16),
+            pltpu.VMEM((N, N // 2), f32),
             pltpu.VMEM((N, N), bf16),
             pltpu.VMEM((DEV, TILES, CH), bf16),
             pltpu.VMEM((2, DEV, TILES, CH), bf16),
             pltpu.SemaphoreType.DMA((4,)),
-            pltpu.SemaphoreType.DMA((4,)),
-            pltpu.SemaphoreType.DMA((2, 5)),
+            pltpu.SemaphoreType.DMA((5,)),
+            pltpu.SemaphoreType.DMA((3, 5)),
         ],
         compiler_params=pltpu.CompilerParams(
             collective_id=0, has_side_effects=True, vmem_limit_bytes=40 << 20

time: 58.6 us -> 57.4 us (0.980)
  Pallas kernels: 57 us -> 55.5 us
    pallas_call x1, Pallas kernels: 57 us -> 55.5 us  [shards(): pl.pallas_call(kernel, out_shape=jax.ShapeDtypeStruct((POS, CH), f32), in...]
where the time goes in v6:
time: 57.4 us; the launch traced here: 56.5 us
  Pallas kernels  55.5 us (97%)
  local copies, waits for them, and re-layouts  0.97 us (2%)
    pallas_call x1, Pallas kernels, shards(): pl.pallas_call(kernel, out_shape=jax.ShapeDtypeStruct((POS, CH), f32), in...  55.5 us

profile of v6, /device:TPU:1, one launch (start us, length us, event | category | flops | bytes accessed | tf_op | source)
XLA Modules:
  0.0 56.5 jit_solution(4417305978355089367)
XLA Ops:
  0.0 55.5 %shard_map.46 = f32[2048,128]{1,0:T(8,128)S(1)} custom-call(f32[2048,128]{1,0:T(8,128)} %bitcast.4, f32[4,128]{1,0:T(4,128)} %bitcast.5, bf16[2,128,640]{2,1,0:T(8,128)(2,1)} %weight_in.1, bf16[2,128,128]{2,1,0:T(8,128)(2,1)} %weight_out_in.1), custom_call_target="tpu_custom_call" | custom-call | tf_op jit(solution)/shard_map/pallas_call | solution.py:342
  55.5 1.0 %copy.6 = f32[64,32,128]{2,1,0:T(8,128)} copy(f32[64,32,128]{2,1,0:T(8,128)S(1)} %bitcast.3) | data formatting | bytes 2097152

commit v7 on v6

--- a/solution.py
+++ b/solution.py
@@ -20,6 +20,7 @@
 STEPS = POS // WIDE
 APART = 40
 CLOSE = 24
+FAR = 136
 PLANE = DEV // 4
 SUB = WIDE // CH
 
@@ -56,7 +57,7 @@
 
 
 def kernel(pair_in, gain_in, weight_in, weight_out_in, out, pair, gain, weight, weight_out, state,
-           normed, gate, wt, wot, gcol, wide, send_a, send_b, send, recv_a, recv_b, recv, xl, xr, xf, turned, tri_send, tri_recv, in_sem,
+           normed, gate, wt, wot, gcol, wide, wide_out, send_a, send_b, send, recv_a, recv_b, recv, xl, xr, xf, turned, tri_send, tri_recv, in_sem,
            send_sem, recv_sem):
     r, c = lax.axis_index("row"), lax.axis_index("col")
     me = r * COLS + c
@@ -131,13 +132,19 @@
             def _():
                 visit(chip, place)
 
-    slot = r * 4 + lax.rem(c, 4)
+    slot = core * PER + r * 2 + lax.div(y, 2)
 
     def spread_channels(g, i, u):
         src, dst = (send_a, recv_a) if u == 0 else (send, recv)
         spread(
             lambda other, place: src.at[(g * 4 + i) * PER + place], dst.at[i * PLANE + slot],
             send_sem.at[2 * u], recv_sem.at[u, i], g, i,
+        )
+
+    def spread_part(g, i, rows, sem):
+        spread(
+            lambda other, place: send.at[(g * 4 + i) * PER + place, rows], recv.at[i * PLANE + slot, rows],
+            send_sem.at[2], recv_sem.at[sem, i], g, i,
         )
 
     def spread_late(g, i):
@@ -218,12 +225,29 @@
                         send_b[at] = second_half.astype(jnp.bfloat16)
             if n == 1 and u == 0:
                 ready()
-            if n % 2 == 1:
+            if n % 2 == 1 and u == 0:
                 for i in range(4):
                     spread_channels(g, i, u)
+            if n % 2 == 1 and u == 1:
+                @pl.when(core == 0)
+                def _():
+                    for i in range(4):
+                        spread_channels(g, i, u)
+
+                @pl.when(core == 1)
+                def _():
+                    for i in range(4):
+                        spread_part(g, i, pl.ds(0, TILES), 1)
+
         if u == 0:
             for n in range(8):
                 spread_late(n // 4, n % 4)
+        else:
+            @pl.when(core == 1)
+            def _():
+                for n in range(8):
+                    spread_part(n // 4, n % 4, pl.ds(TILES, TILES), 3)
+
 
         def open_gate(n, _):
             at = pl.ds(pl.multiple_of(n * WIDE, WIDE), WIDE)
@@ -235,7 +259,7 @@
             turn(1)
         def join_half(src, i, cc, lo, top):
             for m in range(2):
-                v = [src[i * PLANE + (4 * m + q) * 4 + cc, pl.ds(lo, 8), :].astype(jnp.float32) for q in range(4)]
+                v = [src[i * PLANE + cc % 2 * PER + (4 * m + q) * 2 + cc // 2, pl.ds(lo, 8), :].astype(jnp.float32) for q in range(4)]
                 for k in range(4):
                     at = pl.multiple_of(top + cc * B + k * 8, 8)
                     xf[pl.ds(at, 8), m * CH : (m + 1) * CH] = jnp.concatenate(
@@ -244,7 +268,10 @@
 
         def send_half(half):
             for h in range(2):
-                tri = dot(turned[pl.ds(h * CH, CH), :], xl[...]).astype(jnp.bfloat16)
+                if u == 0:
+                    tri = dot(turned[pl.ds(h * CH, CH), :], xl[...]).astype(jnp.bfloat16)
+                else:
+                    tri = dot(xr[pl.ds(half * N // 2 + h * CH, CH), :], turned[...]).astype(jnp.bfloat16)
                 for q in range(4):
                     cc = 2 * (4 * h + q) + half
                     for rp in range(4):
@@ -256,50 +283,42 @@
             for i in range(4):
                 spread_tri(half, i, u)
 
-        for half in range(2 - u):
+        for half in range(2):
             for i, k in enumerate(FAR_FIRST):
-                top = lax.rem(x + 4 - k, 4) * CH
+                far = lax.rem(x + 4 - k, 4)
+                top = far * CH
                 block = pl.ds(pl.multiple_of(top, CH), CH)
                 plane = pl.ds(i * PLANE, PLANE)
-                if u == 1:
-                    arrived(recv.at[plane], recv_sem.at[1, i])
+                if u == 1 and half == 0:
+                    arrived(recv.at[pl.ds(i * PLANE, PLANE * 3 // 4)], recv_sem.at[1, i])
+                elif u == 1:
+                    arrived(recv.at[pl.ds(i * PLANE, PLANE // 4)], recv_sem.at[3, i])
                 elif half == 0:
                     arrived(recv_a.at[plane], recv_sem.at[0, i])
                 else:
                     arrived(recv_b.at[plane], recv_sem.at[2, i])
                 for cc in range(4):
                     at = pl.multiple_of(top + cc * B, B)
-                    place = lambda row: i * PLANE + row * 4 + cc
+                    place = lambda row: i * PLANE + cc % 2 * PER + row * 2 + cc // 2
                     if u == 1:
-                        join_tiles(lambda row: recv[place(row), pl.ds(0, TILES), :], xl, at)
-                        join_tiles(lambda row: recv[place(row), pl.ds(TILES, TILES), :], xr, at)
+                        if half == 0:
+                            join_tiles(lambda row: recv[place(row), pl.ds(0, TILES), :], xl, at)
+                        if cc % 2 == half:
+                            to = pl.multiple_of(half * N // 2 + far * 2 * B + cc // 2 * B, B)
+                            join_tiles(lambda row: recv[place(row), pl.ds(TILES, TILES), :], xr, to)
                     elif half == 0:
                         join_tiles(lambda row: recv_a[place(row), pl.ds(0, TILES), :], xl, at)
                         join_half(recv_a, i, cc, TILES, top)
                     else:
                         join_half(recv_b, i, cc, 0, top)
-                if u == 1:
+                if u == 1 and half == 0:
                     turned[:, block] = jnp.transpose(xl[block, :])
-                else:
+                elif u == 0:
                     turned[0 : N // 2, block] = jnp.transpose(xf[block, :].astype(jnp.bfloat16))
-            if u == 0:
-                send_half(half)
-
-        if u == 1:
-            left(tri_send, 1)
-            for h in range(4):
-                tri = dot(xr[pl.ds(h * CH, CH), :], turned[...]).astype(jnp.bfloat16)
-                for i in range(4):
-                    cc = h * 4 + i
-                    for rp in range(4):
-                        q0 = tri[i * B : i * B + TILES, rp * CH : (rp + 1) * CH]
-                        q1 = tri[i * B + TILES : (i + 1) * B, rp * CH : (rp + 1) * CH]
-                        p0, p1 = swap_halves(q0, q1)
-                        tri_send[2 * rp * COLS + cc] = p0
-                        tri_send[(2 * rp + 1) * COLS + cc] = p1
-            for g in (1, 0):
-                for i in range(4):
-                    spread_tri(g, i, u)
+            if u == 1 and half == 0:
+                left(tri_send, 1)
+            send_half(half)
+
         arrived(tri_recv.at[u], recv_sem.at[u, 4])
 
         def unpack(n, _):
@@ -324,12 +343,19 @@
                 if u == 0:
                     normed[:, pl.ds(pl.multiple_of(n * WIDE + h * CH, CH), CH)] = layer_norm(part, gcol[2]).astype(jnp.bfloat16)
                 else:
-                    rows = jnp.transpose(part)
-                    for p in range(2):
-                        out[pl.ds(p * TILES + n * SUB + h, A, stride=B), :] = rows[p * A : (p + 1) * A]
+                    wide_out[pl.ds(pl.multiple_of((n * SUB + h) * FAR, 8), CH), :] = jnp.transpose(part)
             return 0
 
         lax.fori_loop(0, STEPS, finish, 0, unroll=True)
+
+    def order(a, _):
+        for k in range(4):
+            p, o = k // 2, k % 2
+            to = pl.multiple_of(a * B + k * 8, 8)
+            out[pl.ds(to, 8), :] = wide_out[pl.ds(o * 8 * FAR + p * A + a, 8, stride=FAR), :]
+        return 0
+
+    lax.fori_loop(0, A, order, 0, unroll=16)
     left(send_a, 0)
     left(send_b, 4)
     left(send, 2)
@@ -356,6 +382,7 @@
             pltpu.VMEM((2, CH, CH), bf16),
             pltpu.VMEM((4, CH, CH), f32),
             pltpu.VMEM((CLOSE * CH, CH), f32),
+            pltpu.VMEM((FAR * TILES, CH), f32),
             pltpu.VMEM((DEV, TILES + 8, CH), bf16),
             pltpu.VMEM((DEV, 8, CH), bf16),
             pltpu.VMEM((DEV, 2 * TILES, CH), bf16),
@@ -370,7 +397,7 @@
             pltpu.VMEM((2, DEV, TILES, CH), bf16),
             pltpu.SemaphoreType.DMA((4,)),
             pltpu.SemaphoreType.DMA((5,)),
-            pltpu.SemaphoreType.DMA((3, 5)),
+            pltpu.SemaphoreType.DMA((4, 5)),
         ],
         compiler_params=pltpu.CompilerParams(
             collective_id=0, has_side_effects=True, vmem_limit_bytes=40 << 20

time: 57.4 us -> 56.6 us (0.986); the launches traced: 56.5 us -> 56.5 us
  no operation moved by 1% of the time
where the time goes in v7:
time: 56.6 us; the launch traced here: 56.5 us
  Pallas kernels  55.5 us (98%)
  local copies, waits for them, and re-layouts  0.97 us (2%)
    pallas_call x1, Pallas kernels, shards(): pl.pallas_call(kernel, out_shape=jax.ShapeDtypeStruct((POS, CH), f32), in...  55.5 us

profile of v7, /device:TPU:1, one launch (start us, length us, event | category | flops | bytes accessed | tf_op | source)
XLA Modules:
  0.0 56.5 jit_solution(3255447779724794518)
XLA Ops:
  0.0 55.5 %shard_map.46 = f32[2048,128]{1,0:T(8,128)S(1)} custom-call(f32[2048,128]{1,0:T(8,128)} %bitcast.4, f32[4,128]{1,0:T(4,128)} %bitcast.5, bf16[2,128,640]{2,1,0:T(8,128)(2,1)} %weight_in.1, bf16[2,128,128]{2,1,0:T(8,128)(2,1)} %weight_out_in.1), custom_call_target="tpu_custom_call" | custom-call | tf_op jit(solution)/shard_map/pallas_call | solution.py:368
  55.5 1.0 %copy.6 = f32[64,32,128]{2,1,0:T(8,128)} copy(f32[64,32,128]{2,1,0:T(8,128)S(1)} %bitcast.3) | data formatting | bytes 2097152

commit v8 on v7

--- a/solution.py
+++ b/solution.py
@@ -69,8 +69,7 @@
             ((weight_in, weight), (gain_in, gain), (pair_in, pair), (weight_out_in, weight_out))
         )
     ]
-    for load in loads:
-        load.start()
+    loads[2].start()
 
     x, y, z = lax.div(c, 4), lax.rem(lax.div(c, 2), 2) * 2 + lax.div(r, 4), lax.rem(r, 4)
     mine = (core * 4 + x) * PER + r * 2 + lax.div(y, 2)
@@ -108,6 +107,8 @@
 
     greet(0)
     greet(1)
+    for i in (0, 1, 3):
+        loads[i].start()
     pl.semaphore_signal(barrier, inc=1, device_id=chip * 2 + 1 - core, device_id_type=LOGICAL)
 
     def ready():

time: 56.6 us -> 56 us (0.989)
  Pallas kernels: 55.5 us -> 54.9 us
    pallas_call x1, Pallas kernels: 55.5 us -> 54.9 us  [shards(): pl.pallas_call(kernel, out_shape=jax.ShapeDtypeStruct((POS, CH), f32), in...]
where the time goes in v8:
time: 56 us; the launch traced here: 55.9 us
  Pallas kernels  54.9 us (98%)
  local copies, waits for them, and re-layouts  0.97 us (2%)
    pallas_call x1, Pallas kernels, shards(): pl.pallas_call(kernel, out_shape=jax.ShapeDtypeStruct((POS, CH), f32), in...  54.9 us

profile of v8, /device:TPU:1, one launch (start us, length us, event | category | flops | bytes accessed | tf_op | source)
XLA Modules:
  0.0 55.9 jit_solution(17745560642965026848)
XLA Ops:
  0.0 54.9 %shard_map.46 = f32[2048,128]{1,0:T(8,128)S(1)} custom-call(f32[2048,128]{1,0:T(8,128)} %bitcast.4, f32[4,128]{1,0:T(4,128)} %bitcast.5, bf16[2,128,640]{2,1,0:T(8,128)(2,1)} %weight_in.1, bf16[2,128,128]{2,1,0:T(8,128)(2,1)} %weight_out_in.1), custom_call_target="tpu_custom_call" | custom-call | tf_op jit(solution)/shard_map/pallas_call | solution.py:369
  54.9 1.0 %copy.6 = f32[64,32,128]{2,1,0:T(8,128)} copy(f32[64,32,128]{2,1,0:T(8,128)S(1)} %bitcast.3) | data formatting | bytes 2097152
